TPU v7x, 128 devices: a whole 4x4x4 slice. The times are simulated.
128 devices in a mesh: vtx: 32 (over z, x, core), feat: 4 (over y).
Axes of the slice: x: 4, y: 4, z: 4, core: 2. Of those that a mesh axis runs over, the one named last changes fastest.
Arguments:
- features: bfloat16 [131072, 768], P('vtx', 'feat'), may hold values from -6 to 6
- w_self: bfloat16 [768, 256], P('feat'), may hold values from -0.21875 to 0.21875
- w_neigh: bfloat16 [768, 256], P('feat'), may hold values from -0.21875 to 0.21875
- bias_terms: float32 [256], P('feat'), may hold values from -3 to 3
- block_vals: bfloat16 [10240, 128, 128], P('vtx'), may hold values from 0 to 1
- block_rows: int32 [10240], P('vtx'), may hold values from 0 to 31, as said below
- block_cols: int32 [10240], P('vtx'), may hold values from 0 to 63, as said below
- block_count: int32 [32], P('vtx'), may hold values from 1 to 320, as said below
- recv_lists: int32 [1024], P('vtx'), may hold values from -1 to 31, as said below
- degree: int32 [131072], P('vtx'), may hold values from 8 to 63
- cotangent: bfloat16 [131072, 256], P('vtx', 'feat'), may hold values from -6 to 6
Outputs:
- hidden: bfloat16 [131072, 256], P('vtx', 'feat')
- grad_features: bfloat16 [131072, 768], P('vtx', 'feat')
- grad_self: float32 [768, 256], P('feat')
- grad_neigh: float32 [768, 256], P('feat')
Inputs may be any that keep to these rules, and one draw needn't show every extreme that they name: Entry e of a shard's list adds into the shard's own row block block_rows[e]. `block_cols`: an index into the shard's extended list: 16 left slots, its 32 own blocks, 16 right slots. `block_count`: the live entries of a shard's list come first and entries past its count are ignored; some shard has all 320 entries live. `recv_lists`: per shard 2 * 16 slots: distinct blocks of the left neighbour, then distinct blocks of the right neighbour; live slots come first, the others and all slots toward a missing neighbour are -1; some shard has 16 live right slots.
All inputs are finite; a program needn't handle non-finite values.
Results may differ from a plain program's by a relative error of at most 0.0053.
Values may be sent and summed in bfloat16 or wider, within the bound.
A program may use at most 192 MiB of HBM per device.

v0:
```python
import jax
import jax.numpy as jnp
from jax import lax
from jax.sharding import PartitionSpec as P


def padded_2(array, sides, width):
    for axis, dim in sides:
        size, length = (lax.axis_size(axis), array.shape[dim])
        up = [(i, (i + 1) % size) for i in range(size - 1)]
        down = [(j, i) for i, j in up]
        last = lax.slice_in_dim(array, length - width, length, axis=dim)
        initial = lax.slice_in_dim(array, 0, width, axis=dim)
        before = lax.ppermute(last, axis, up)
        after = lax.ppermute(initial, axis, down)
        array = jnp.concatenate([before, array, after], axis=dim)
    return array


def gather_blocks(source, wanted):
    picked = source[jnp.clip(wanted, 0)]
    return jnp.where((wanted >= 0)[:, None, None], picked, jnp.zeros_like(picked))


def add_by_index(incoming, index, count):
    selector = (index[None, :] == jnp.arange(count, dtype=jnp.int32)[:, None]).astype(jnp.float32)
    flat = incoming.reshape(incoming.shape[0], -1)
    summed = jnp.dot(
        selector, flat, precision=lax.Precision.HIGHEST, preferred_element_type=jnp.float32
    )
    return summed.reshape((count,) + incoming.shape[1:])


def on_device(
    features,
    w_self,
    w_neigh,
    bias_terms,
    block_vals,
    block_rows,
    block_cols,
    block_count,
    recv_lists,
    degree,
    cotangent,
):
    row_count, feat_cols = features.shape
    block_size = block_vals.shape[1]
    home_count = row_count // block_size
    halo_slots = recv_lists.shape[0] // 2
    home = features.reshape(home_count, block_size, feat_cols)
    left_wanted = recv_lists[:halo_slots]
    right_wanted = recv_lists[halo_slots:]
    padded = padded_2(features, (("vtx", 0),), row_count)
    padded = padded.reshape(3 * home_count, block_size, feat_cols)
    from_left = gather_blocks(padded[:home_count], left_wanted)
    from_right = gather_blocks(padded[2 * home_count :], right_wanted)
    extended = jnp.concatenate([from_left, home, from_right], axis=0)
    active = jnp.arange(block_cols.shape[0], dtype=jnp.int32) < block_count[0]
    weights = jnp.where(active[:, None, None], block_vals, jnp.zeros_like(block_vals))
    operand = extended[block_cols]
    products = jnp.einsum("nij,njf->nif", weights, operand, preferred_element_type=jnp.float32)
    summed = add_by_index(products, block_rows, home_count)
    divisor = degree.astype(jnp.float32)[:, None]
    neighbour_mean = (summed.reshape(row_count, feat_cols) / divisor).astype(jnp.bfloat16)
    partial_pre = jnp.dot(features, w_self, preferred_element_type=jnp.float32) + jnp.dot(
        neighbour_mean, w_neigh, preferred_element_type=jnp.float32
    )
    preact = (
        lax.psum_scatter(partial_pre, "feat", scatter_dimension=1, tiled=True) + bias_terms[None, :]
    )
    squash = jax.nn.sigmoid(preact)
    hidden = (preact * squash).astype(jnp.bfloat16)
    slopes = (cotangent.astype(jnp.float32) * squash * (1.0 + preact * (1.0 - squash))).astype(
        jnp.bfloat16
    )
    slopes_full = lax.all_gather(slopes, "feat", axis=1, tiled=True)
    node_total = row_count * lax.axis_size("vtx")
    factor = float(node_total) ** (-0.5)
    contract_rows = (((0,), (0,)), ((), ()))
    part_self = lax.dot_general(
        features, slopes_full, contract_rows, preferred_element_type=jnp.float32
    )
    part_neigh = lax.dot_general(
        neighbour_mean, slopes_full, contract_rows, preferred_element_type=jnp.float32
    )
    grad_self, grad_neigh = lax.psum((part_self, part_neigh), "vtx")
    grad_self = grad_self * factor
    grad_neigh = grad_neigh * factor
    contract_cols = (((1,), (1,)), ((), ()))
    direct = lax.dot_general(slopes_full, w_self, contract_cols, preferred_element_type=jnp.float32)
    back_mean = (
        lax.dot_general(slopes_full, w_neigh, contract_cols, preferred_element_type=jnp.float32)
        / divisor
    ).astype(jnp.bfloat16)
    source = back_mean.reshape(home_count, block_size, feat_cols)[block_rows]
    block_terms = jnp.einsum("nji,njf->nif", weights, source, preferred_element_type=jnp.float32)
    spread = add_by_index(block_terms, block_cols, home_count + 2 * halo_slots)
    toward_left = spread[:halo_slots]
    home_sum = spread[halo_slots : halo_slots + home_count]
    toward_right = spread[halo_slots + home_count :]
    full_left = add_by_index(toward_left, left_wanted, home_count)
    full_right = add_by_index(toward_right, right_wanted, home_count)
    outbound = jnp.concatenate([full_left, full_right], axis=0).reshape(2 * row_count, feat_cols)
    returned = padded_2(outbound, (("vtx", 0),), row_count)
    home_sum = home_sum + returned[:row_count].reshape(home_count, block_size, feat_cols)
    home_sum = home_sum + returned[3 * row_count :].reshape(home_count, block_size, feat_cols)
    grad_features = (direct + home_sum.reshape(row_count, feat_cols)).astype(jnp.bfloat16)
    return (hidden, grad_features, grad_self, grad_neigh)


def solution(mesh):
    placed = (
        P("vtx", "feat"),
        P("feat", None),
        P("feat", None),
        P("feat"),
        P("vtx", None, None),
        P("vtx"),
        P("vtx"),
        P("vtx"),
        P("vtx"),
        P("vtx"),
        P("vtx", "feat"),
    )
    return jax.shard_map(
        on_device,
        mesh=mesh,
        in_specs=placed,
        out_specs=(P("vtx", "feat"), P("vtx", "feat"), P("feat", None), P("feat", None)),
        check_vma=False,
    )
```

profile of v0, /device:TPU:1, one launch (start us, length us, event | category | flops | bytes accessed | tf_op | source)
XLA Modules:
  0.0 479.1 jit_solution(2182423101184916518)
XLA Ops:
  7.3 4.6 collective-permute-start
  18.0 3.0 copy_bitcast_fusion.4
  21.0 2.8 fusion.19
  23.8 5.8 %collective-permute-done = bf16[4096,192]{0,1:T(8,128)(2,1)S(1)} collective-permute-done((bf16[4096,192]{0,1:T(8,128)(2,1)}, bf16[4096,192]{0,1:T(8,128)(2,1)S(1)}, u32[]{:S(2)}, u32[]{:S(2)}) %collective-permute-start) | collective-permute-done | bytes 1572896 | tf_op jit(solution)/shard_map/ppermute | solution.py:14
  30.7 3.3 collective-permute-done.1
  38.8 12.6 %gather_fusion.2 = bf16[320,128,192]{1,2,0:T(8,128)(2,1)} fusion(bf16[64,128,192]{1,2,0:T(8,128)(2,1)S(1)} %pad_maximum_fusion, s32[1024]{0:T(1024)S(1)} %pad_clamp_fusion.1), kind=kCustom, calls=%fused_computation.2 | custom fusion | bytes 31458560 | tf_op jit(solution)/shard_map/gather | solution.py:61
  51.4 21.7 %fusion.2 = f32[320,128,192]{1,2,0:T(8,128)} fusion(bf16[320,128,192]{1,2,0:T(8,128)(2,1)} %gather_fusion.2, bf16[320,128,128]{2,1,0:T(8,128)(2,1)} %param.15, pred[320]{0:T(512)(128)(4,1)S(1)} %iota_compare_fusion.6), kind=kOutput, calls=%fused_computation.9 | convolution fusion | flops 2018508800 | bytes 57672000 | tf_op jit(solution)/shard_map/nij,njf->nif/dot_general | solution.py:62
  73.1 34.5 %copy.28 = f32[320,128,192]{0,2,1:T(8,128)} copy(f32[320,128,192]{1,2,0:T(8,128)} %fusion.2) | data formatting | bytes 62914560 | tf_op jit(solution)/shard_map/nij,njf->nif/dot_general | solution.py:62
  107.7 24.3 %fusion.6 = f32[32,24576]{1,0:T(8,128)S(1)} fusion(f32[320,24576]{0,1:T(8,128)} %bitcast.72, s32[320]{0:T(512)S(1)} %copy-done.13), kind=kOutput, calls=%fused_computation.34 | convolution fusion | flops 3019909120 | bytes 34604288 | tf_op jit(solution)/shard_map/dot_general | solution.py:28
  131.9 3.4 reshape_reshape.3
  135.4 5.2 %copy.29 = f32[4096,192]{0,1:T(8,128)} copy(f32[4096,192]{1,0:T(8,128)} %reshape_reshape.3) | data formatting | bytes 6291456 | tf_op jit(solution)/shard_map/reshape;reshape | solution.py:65
  146.6 50.6 %reduce-scatter.2.cloned.1.call-done = f32[4096,64]{0,1:T(8,128)} async-done(((f32[4096,256]{0,1:T(8,128)}), f32[4096,64]{0,1:T(8,128)}) %reduce-scatter.2.cloned.1.call-update) | async-done | bytes 1048592 | tf_op jit(solution)/shard_map/reduce_scatter | solution.py:70
  200.1 30.6 %all-gather.2.cloned.1.call-done = bf16[4096,256]{0,1:T(8,128)(2,1)} async-done(((bf16[4096,64]{0,1:T(8,128)(2,1)}), bf16[4096,256]{0,1:T(8,128)(2,1)}) %all-gather.2.cloned.1.call-update) | async-done | bytes 2097168 | tf_op jit(solution)/shard_map/all_gather | solution.py:77
  233.3 12.6 %gather_fusion.3 = bf16[320,128,192]{1,2,0:T(8,128)(2,1)} fusion(bf16[32,128,192]{1,2,0:T(8,128)(2,1)S(1)} %bitcast.70, s32[1024]{0:T(1024)S(1)} %pad_clamp_fusion), kind=kCustom, calls=%fused_computation.3 | custom fusion | bytes 31458560 | tf_op jit(solution)/shard_map/gather | solution.py:96
  245.9 20.4 %fusion.1 = f32[320,128,192]{1,2,0:T(8,128)} fusion(bf16[320,128,192]{1,2,0:T(8,128)(2,1)} %gather_fusion.3, bf16[320,128,128]{2,1,0:T(8,128)(2,1)} %param.15, pred[320]{0:T(512)(128)(4,1)S(1)} %iota_compare_fusion.6), kind=kOutput, calls=%fused_computation.8 | convolution fusion | flops 2018508800 | bytes 57672000 | tf_op jit(solution)/shard_map/nji,njf->nif/dot_general | solution.py:97
  266.2 34.5 %copy.31 = f32[320,128,192]{0,2,1:T(8,128)} copy(f32[320,128,192]{1,2,0:T(8,128)} %fusion.1) | data formatting | bytes 62914560 | tf_op jit(solution)/shard_map/nji,njf->nif/dot_general | solution.py:97
  300.7 25.4 %fusion.4 = f32[64,24576]{1,0:T(8,128)S(1)} fusion(f32[320,24576]{0,1:T(8,128)} %bitcast.71, s32[320]{0:T(512)S(1)} %copy-done.14), kind=kOutput, calls=%fused_computation.31 | convolution fusion | flops 6039818240 | bytes 37750016 | tf_op jit(solution)/shard_map/dot_general | solution.py:28
  335.4 4.4 copy.48
  339.8 3.7 collective-permute-start.2
  349.4 4.4 copy.47
  361.3 3.2 slice.41
  364.5 5.5 %copy.33 = f32[4096,192]{0,1:T(8,128)} copy(f32[4096,192]{1,0:T(8,128)} %slice.41) | data formatting | bytes 6291456 | tf_op jit(solution)/shard_map/slice | solution.py:100
  370.0 93.4 %all-reduce.3.cloned.1.call-done = (f32[192,256]{1,0:T(8,128)}, f32[192,256]{1,0:T(8,128)}) async-done(((f32[192,256]{1,0:T(8,128)}, f32[192,256]{1,0:T(8,128)}), (f32[192,256]{1,0:T(8,128)}, f32[192,256]{1,0:T(8,128)})) %all-reduce.3.cloned.1.call-update) | async-done | bytes 393232 | tf_op jit(solution)/shard_map/psum | solution.py:87
  466.6 5.8 %add_convert_fusion = bf16[4096,192]{0,1:T(8,128)(2,1)} fusion(f32[4096,192]{0,1:T(8,128)} %collective-permute-done.3, f32[4096,192]{0,1:T(8,128)} %copy.33, f32[4096,192]{0,1:T(8,128)} %collective-permute-done.2, bf16[192,256]{1,0:T(8,128)(2,1)S(1)} %copy-done.12, bf16[4096,256]{0,1:T(8,128)(2,1)S(1)} %copy-done.7), kind=kOutput, calls=%fused_computation.13 | convolution fusion | flops 405798912 | bytes 13205504 | tf_op jit(solution)/shard_map/dot_general | solution.py:91
  (78 shorter events, 48.5 us)
Async XLA Ops:
  7.2 135.8 %copy-start = (bf16[192,256]{1,0:T(8,128)(2,1)S(1)}, bf16[192,256]{1,0:T(8,128)(2,1)}, u32[]{:S(2)}) copy-start(bf16[192,256]{1,0:T(8,128)(2,1)} %param.13) | copy-start | bytes 294916
  7.2 13.8 %copy-start.4 = (bf16[4096,192]{0,1:T(8,128)(2,1)S(1)}, bf16[4096,192]{0,1:T(8,128)(2,1)}, u32[]{:S(2)}) copy-start(bf16[4096,192]{0,1:T(8,128)(2,1)} %param.11) | copy-start | bytes 4718596
  7.2 13.8 %copy-start.11 = (bf16[192,256]{1,0:T(8,128)(2,1)S(1)}, bf16[192,256]{1,0:T(8,128)(2,1)}, u32[]{:S(2)}) copy-start(bf16[192,256]{1,0:T(8,128)(2,1)} %param.12) | copy-start | bytes 294916
  7.2 190.0 %reduce-scatter.2.cloned.1.call-start = ((), (), s32[]{:S(2)}) async-start(), calls=%async_computation.1 | async-start | bytes 5242880 | tf_op jit(solution)/shard_map/reduce_scatter | solution.py:70
  7.3 22.3 %collective-permute-start = (bf16[4096,192]{0,1:T(8,128)(2,1)}, bf16[4096,192]{0,1:T(8,128)(2,1)S(1)}, u32[]{:S(2)}, u32[]{:S(2)}) collective-permute-start(bf16[4096,192]{0,1:T(8,128)(2,1)} %param.11), channel_id=1, source_target_pairs={{0,4},{4,8},{8,12},{12,16},{16,20},{20,24},{24,28},{28,32},{32,36}... | collective-permute-start | bytes 4718600 | tf_op jit(solution)/shard_map/ppermute | solution.py:14
  11.9 22.1 %collective-permute-start.1 = (bf16[4096,192]{0,1:T(8,128)(2,1)}, bf16[4096,192]{0,1:T(8,128)(2,1)}, u32[]{:S(2)}, u32[]{:S(2)}) collective-permute-start(bf16[4096,192]{0,1:T(8,128)(2,1)} %param.11), channel_id=1, source_target_pairs={{4,0},{8,4},{12,8},{16,12},{20,16},{24,20},{28,24},{32,28},{36,32}... | collective-permute-start | bytes 4718600 | tf_op jit(solution)/shard_map/ppermute | solution.py:15
  73.1 34.5 %copy-start.13 = (s32[320]{0:T(512)S(1)}, s32[320]{0:T(512)}, u32[]{:S(2)}) copy-start(s32[320]{0:T(512)} %param.16) | copy-start | bytes 3844
  140.6 3.1 copy-start.2
  146.5 50.7 %copy-start.10 = (bf16[4096,64]{0,1:T(8,128)(2,1)S(1)}, bf16[4096,64]{0,1:T(8,128)(2,1)}, u32[]{:S(2)}) copy-start(bf16[4096,64]{0,1:T(8,128)(2,1)} %param.21) | copy-start | bytes 1572868
  146.5 50.7 %copy-start.16 = (f32[64]{0:T(128)S(1)}, f32[64]{0:T(128)}, u32[]{:S(2)}) copy-start(f32[64]{0:T(128)} %param.14) | copy-start | bytes 772
  146.6 84.1 %all-gather.2.cloned.1.call-start = ((), (), s32[]{:S(2)}) async-start(), calls=%async_computation.2 | async-start | bytes 2621440 | tf_op jit(solution)/shard_map/all_gather | solution.py:77
  200.0 263.4 %all-reduce.3.cloned.1.call-start = ((), (), s32[]{:S(2)}) async-start(), calls=%async_computation.3 | async-start | bytes 786432 | tf_op jit(solution)/shard_map/psum | solution.py:87
  266.2 34.5 %copy-start.14 = (s32[320]{0:T(512)S(1)}, s32[320]{0:T(512)}, u32[]{:S(2)}) copy-start(s32[320]{0:T(512)} %param.17) | copy-start | bytes 3844
  326.1 3.1 copy-start.3
  335.4 8.1 %copy-start.8 = (f32[24576,16]{0,1:T(8,128)S(1)}, f32[24576,16]{0,1:T(8,128)}, u32[]{:S(2)}) copy-start(f32[24576,16]{0,1:T(8,128)} %get-tuple-element.7) | copy-start | bytes 4718596
  339.8 126.8 %collective-permute-start.2 = (f32[4096,192]{0,1:T(8,128)}, f32[4096,192]{0,1:T(8,128)}, u32[]{:S(2)}, u32[]{:S(2)}) collective-permute-start(f32[4096,192]{0,1:T(8,128)} %bitcast.67), channel_id=1, source_target_pairs={{0,4},{4,8},{8,12},{12,16},{16,20},{20,24},{24,28},{28,32},{32,36}... | collective-permute-start | bytes 9437192 | tf_op jit(solution)/shard_map/ppermute | solution.py:14
  343.5 4.3 copy-start.15
  349.4 6.9 %copy-start.6 = (bf16[4096,256]{0,1:T(8,128)(2,1)S(1)}, bf16[4096,256]{0,1:T(8,128)(2,1)}, u32[]{:S(2)}) copy-start(bf16[4096,256]{0,1:T(8,128)(2,1)} %all-gather.2.cloned.1.call-done) | copy-start | bytes 6291460
  353.8 4.0 copy-start.5
  353.8 112.8 %collective-permute-start.3 = (f32[4096,192]{0,1:T(8,128)}, f32[4096,192]{0,1:T(8,128)}, u32[]{:S(2)}, u32[]{:S(2)}) collective-permute-start(f32[4096,192]{0,1:T(8,128)} %bitcast.66), channel_id=1, source_target_pairs={{4,0},{8,4},{12,8},{16,12},{20,16},{24,20},{28,24},{32,28},{36,32}... | collective-permute-start | bytes 9437192 | tf_op jit(solution)/shard_map/ppermute | solution.py:15
  359.4 1.9 slice-start
  364.5 102.1 %copy-start.7 = (bf16[4096,256]{0,1:T(8,128)(2,1)S(1)}, bf16[4096,256]{0,1:T(8,128)(2,1)}, u32[]{:S(2)}) copy-start(bf16[4096,256]{0,1:T(8,128)(2,1)} %all-gather.2.cloned.1.call-done) | copy-start | bytes 6291460
  364.5 102.1 %copy-start.12 = (bf16[192,256]{1,0:T(8,128)(2,1)S(1)}, bf16[192,256]{1,0:T(8,128)(2,1)}, u32[]{:S(2)}) copy-start(bf16[192,256]{1,0:T(8,128)(2,1)} %param.12) | copy-start | bytes 294916
  466.6 5.8 %copy-start.1 = (bf16[192,256]{1,0:T(8,128)(2,1)S(1)}, bf16[192,256]{1,0:T(8,128)(2,1)}, u32[]{:S(2)}) copy-start(bf16[192,256]{1,0:T(8,128)(2,1)} %param.13) | copy-start | bytes 294916
  (1 other events, 1.4 us)
Sparse Core Ops, SparseCore 0:
  146.7 50.4 reduce-scatter.1
  200.1 30.4 all-gather.1
  359.5 103.7 all-reduce.2
where the time goes:
time: 484 us; the launch traced here: 479 us
  waiting for transfers between devices  184 us (38%)
  local copies, waits for them, and re-layouts  144 us (30%)
  matrix products  111 us (23%)
  between operations  15 us (3%)
  starting transfers between devices  12.8 us (3%)
  other arithmetic  12.8 us (3%)
    psum x1, waiting for transfers between devices, on_device(): grad_self, grad_neigh = lax.psum((part_self, part_neigh), 'vtx')  93.4 us
    dot_general x4, matrix products, add_by_index(): jnp.dot(selector, flat, precision=lax.Precision.HIGHEST, preferred_elemen...  52.7 us
    reduce_scatter x1, waiting for transfers between devices, on_device(): lax.psum_scatter(partial_pre, 'feat', scatter_dimension=1, tiled=True)  50.6 us
    dot_general x1, local copies, waits for them, and re-layouts, on_device(): jnp.einsum('nij,njf->nif', weights, operand, preferred_element_type=jnp.f...  34.5 us
    dot_general x1, local copies, waits for them, and re-layouts, on_device(): jnp.einsum('nji,njf->nif', weights, source, preferred_element_type=jnp.fl...  34.5 us
    all_gather x1, waiting for transfers between devices, on_device(): slopes_full = lax.all_gather(slopes, 'feat', axis=1, tiled=True)  30.6 us
    dot_general x1, matrix products, on_device(): jnp.einsum('nij,njf->nif', weights, operand, preferred_element_type=jnp.f...  21.7 us
    dot_general x1, matrix products, on_device(): jnp.einsum('nji,njf->nif', weights, source, preferred_element_type=jnp.fl...  20.4 us
  transfers between devices with their start and end apart: 7, of which 5 were waited for; matrix products, arithmetic and copies ran while one was open for 7% of the time, Pallas kernels for 0%

commit v1 on v0

v1 whole, which is shorter than its diff:
```python
import functools

import jax
import jax.numpy as jnp
from jax import lax
from jax.experimental import pallas as pl
from jax.experimental.pallas import tpu as pltpu
from jax.sharding import PartitionSpec as P

MESH = pl.DeviceIdType.MESH
F32, BF16, I32 = jnp.float32, jnp.bfloat16, jnp.int32
BS = 128
NB = 32
HALO = 16
NNZ = 320
EXT = NB + 2 * HALO
FC = 192
HID = 256
HC = 64
ROWS = NB * BS
NV, NF = 32, 4
ENT = 384
PIECES = 8
PW = ROWS // PIECES
MB = 1 << 20


def vmem():
    return pl.BlockSpec(memory_space=pltpu.VMEM)


def smem():
    return pl.BlockSpec(memory_space=pltpu.SMEM)


def anyspace():
    return pl.BlockSpec(memory_space=pl.ANY)


def greet(peers):
    barrier = pltpu.get_barrier_semaphore()
    for peer in peers:
        pl.semaphore_signal(barrier, inc=1, device_id=peer, device_id_type=MESH)
    pl.semaphore_wait(barrier, len(peers))


def iota(shape, dim):
    return lax.broadcasted_iota(I32, shape, dim).astype(F32)


def as_column(row):
    n = row.shape[1]
    diagonal = iota((n, n), 0) == iota((n, n), 1)
    return jnp.sum(jnp.where(diagonal, row, 0.0), axis=1, keepdims=True)


def pair_schedule(key, other, active):
    far = 1000.0
    sub, lane = iota((ENT, ENT), 0), iota((ENT, ENT), 1)
    key = jnp.where(active, key, far)
    key_col = as_column(key)
    rank = jnp.sum(jnp.where((key_col == key) & (sub < lane), 1.0, 0.0), axis=0, keepdims=True)
    group = iota((EXT, ENT), 0)
    size = jnp.sum(jnp.where(group == key, 1.0, 0.0), axis=1, keepdims=True)
    size = 2.0 * jnp.floor((size + 1.0) * 0.5)
    start = jnp.sum(jnp.where(group < key, size, 0.0), axis=0, keepdims=True)
    slot = jnp.where(active, start + rank, far)
    slot_col = as_column(slot)
    hit = slot_col == lane

    def at_slots(column, default):
        return jnp.sum(jnp.where(hit, column - default, 0.0), axis=0, keepdims=True) + default

    entry = at_slots(sub[:, :1], float(NNZ))
    source = at_slots(as_column(other), 0.0)
    target = at_slots(key_col, float(EXT))
    used = jnp.broadcast_to(jnp.sum(size, axis=0, keepdims=True), (1, ENT))
    return entry, source, target, used


def halo_kernel(table_ref, lists_ref, feat_ref, halo_ref, plan_ref, lists_in, lists_sm, blocks, sent, sm_sem, ls, lr, bs, br):
    me = lax.axis_index("vtx")
    right, left = lax.rem(me + 1, NV), lax.rem(me + NV - 1, NV)
    greet([{"vtx": left}, {"vtx": right}])
    trips = []
    for k, peer in ((0, right), (1, left)):
        trip = pltpu.make_async_remote_copy(
            src_ref=lists_ref, dst_ref=lists_in.at[k], send_sem=ls.at[k], recv_sem=lr.at[k],
            device_id={"vtx": peer}, device_id_type=MESH,
        )
        trip.start()
        trips.append(trip)
    blocks[0] = jnp.zeros((FC, BS), BF16)
    for b in range(NB):
        blocks[1 + b] = feat_ref[:, b * BS : (b + 1) * BS]
    for trip in trips:
        trip.wait()
    local = pltpu.make_async_copy(lists_in, lists_sm, sm_sem)
    local.start()
    local.wait()
    sends = []
    for part in range(4):
        for d in range(2):
            for j in range(4 * part, 4 * part + 4):
                sent[d, j] = blocks[lists_sm[1 - d, 0, j + HALO * d] + 1]
            trip = pltpu.make_async_remote_copy(
                src_ref=sent.at[d, pl.ds(4 * part, 4)], dst_ref=halo_ref.at[d, pl.ds(4 * part, 4)],
                send_sem=bs.at[d, part], recv_sem=br.at[d, part],
                device_id={"vtx": right if d == 0 else left}, device_id_type=MESH,
            )
            trip.start()
            sends.append(trip)
    table = table_ref[...].astype(F32)
    rows, cols, count = table[0:1], table[1:2], table[2:3]
    active = iota((1, ENT), 1) < count
    forward = pair_schedule(rows, cols, active)
    backward = pair_schedule(cols, rows, active)

    def inverse(lists, first):
        ours = as_column(lists)
        sub, lane = iota((BS, BS), 0), iota((BS, BS), 1)
        hit = (ours == lane) & (sub >= first) & (sub < first + HALO)
        return jnp.sum(jnp.where(hit, sub - (first + HALO), 0.0), axis=0, keepdims=True) + float(HALO)

    from_right = inverse(lists_in[1, 0:1].astype(F32), 0)
    from_left = inverse(lists_in[0, 0:1].astype(F32), HALO)
    last = jnp.concatenate([from_right, from_left, jnp.zeros((1, BS), F32)], axis=1)
    used = jnp.where(iota((1, ENT), 1) < 192.0, forward[3], backward[3])
    plan = forward[:3] + backward[:3] + (last, used)
    for k, row in enumerate(plan):
        plan_ref[k : k + 1] = row.astype(I32)
    for trip in sends:
        trip.wait()


def halo_call(table, lists, feat):
    return pl.pallas_call(
        halo_kernel,
        out_shape=(
            jax.ShapeDtypeStruct((2, HALO, FC, BS), BF16),
            jax.ShapeDtypeStruct((8, ENT), I32),
        ),
        in_specs=[vmem()] * 3,
        out_specs=(anyspace(), vmem()),
        scratch_shapes=[
            pltpu.VMEM((2, 8, BS), I32),
            pltpu.SMEM((2, 8, BS), I32),
            pltpu.VMEM((NB + 1, FC, BS), BF16),
            pltpu.VMEM((2, HALO, FC, BS), BF16),
            pltpu.SemaphoreType.DMA,
            pltpu.SemaphoreType.DMA((2,)),
            pltpu.SemaphoreType.DMA((2,)),
            pltpu.SemaphoreType.DMA((2, 4)),
            pltpu.SemaphoreType.DMA((2, 4)),
        ],
        compiler_params=pltpu.CompilerParams(collective_id=0, has_side_effects=True, vmem_limit_bytes=48 * MB),
        name="halo_out",
    )(table, lists, feat)


GROUP = 8


def load_vals(vals_hbm, vals, sems):
    share = NNZ // 8
    loads = [
        pltpu.make_async_copy(vals_hbm.at[pl.ds(k * share, share)], vals.at[pl.ds(k * share, share)], sems.at[k])
        for k in range(8)
    ]
    for load in loads:
        load.start()
    vals[NNZ] = jnp.zeros((BS, BS), BF16)
    return loads


def forward_kernel(plan, vals_hbm, feat_ref, halo_ref, degree_ref, mean_ref, vals, ext, acc, sems):
    loads = load_vals(vals_hbm, vals, sems)
    for j in range(HALO):
        ext[j] = halo_ref[0, j]
        ext[HALO + NB + j] = halo_ref[1, j]
    for b in range(NB):
        ext[HALO + b] = feat_ref[:, b * BS : (b + 1) * BS]
    acc[...] = jnp.zeros_like(acc)
    for load in loads:
        load.wait()

    @pl.loop(0, (plan[7, 0] + 2 * GROUP - 1) // (2 * GROUP))
    def _(step):
        for u in range(GROUP):
            slot = step * (2 * GROUP) + 2 * u
            a = jnp.concatenate([vals[plan[0, slot]], vals[plan[0, slot + 1]]], axis=1)
            x = jnp.concatenate([ext[plan[1, slot]], ext[plan[1, slot + 1]]], axis=1)
            row = jnp.minimum(plan[2, slot], NB)
            acc[row] += lax.dot_general(x, a, (((1,), (1,)), ((), ())), preferred_element_type=F32)

    for b in range(NB):
        divisor = degree_ref[b : b + 1, :].astype(F32)
        mean_ref[:, b * BS : (b + 1) * BS] = (acc[b] / divisor).astype(BF16)


def forward_call(plan, vals, feat, halo, degree):
    return pl.pallas_call(
        forward_kernel,
        out_shape=jax.ShapeDtypeStruct((FC, ROWS), BF16),
        in_specs=[smem(), anyspace(), vmem(), vmem(), vmem()],
        out_specs=vmem(),
        scratch_shapes=[
            pltpu.VMEM((NNZ + 1, BS, BS), BF16),
            pltpu.VMEM((EXT, FC, BS), BF16),
            pltpu.VMEM((NB + 1, FC, BS), F32),
            pltpu.SemaphoreType.DMA((8,)),
        ],
        compiler_params=pltpu.CompilerParams(vmem_limit_bytes=48 * MB),
        name="sparse_forward",
    )(plan, vals, feat, halo, degree)


def dense_kernel(
    feat_ref, mean_ref, cot_ref, ws_ref, wn_ref, wst_ref, wnt_ref, bias_ref, degree_ref,
    hidden_ref, back_ref, direct_ref, grads_ref,
    part, staged, landed, slopes, total, send_sem, recv_sem,
):
    me = lax.axis_index("feat")
    right, left = lax.rem(me + 1, NF), lax.rem(me + NF - 1, NF)
    greet([{"feat": left}, {"feat": right}])

    half = PIECES // 2
    order = [p for k in range(half) for p in (k, half + k)]
    way = {p: (1 if p < half else -1) for p in order}
    peer = {1: right, -1: left}

    def cols(p):
        return slice(p * PW, (p + 1) * PW)

    def chunk(p, back):
        return lax.rem(me - way[p] * back + 2 * NF, NF)

    def reduce_hop(p, s):
        return pltpu.make_async_remote_copy(
            src_ref=staged.at[s, p], dst_ref=landed.at[s, p],
            send_sem=send_sem.at[s, p], recv_sem=recv_sem.at[s, p],
            device_id={"feat": peer[way[p]]}, device_id_type=MESH,
        )

    def gather_hop(p, s):
        owner = chunk(p, s)
        return pltpu.make_async_remote_copy(
            src_ref=slopes.at[p, owner], dst_ref=slopes.at[p, owner],
            send_sem=send_sem.at[3 + s, p], recv_sem=recv_sem.at[3 + s, p],
            device_id={"feat": peer[way[p]]}, device_id_type=MESH,
        )

    hops = {}
    for p in order:
        pre = jnp.dot(wst_ref[...], feat_ref[:, cols(p)], preferred_element_type=F32)
        pre += jnp.dot(wnt_ref[...], mean_ref[:, cols(p)], preferred_element_type=F32)
        part[p] = pre.reshape(NF, HC, PW)
        staged[0, p] = part[p, chunk(p, 1)].astype(BF16)
        hops[0, p] = reduce_hop(p, 0)
        hops[0, p].start()
    for s in range(1, 3):
        for p in order:
            hops[s - 1, p].wait_recv()
            staged[s, p] = (landed[s - 1, p].astype(F32) + part[p, chunk(p, 1 + s)]).astype(BF16)
            hops[s, p] = reduce_hop(p, s)
            hops[s, p].start()
    for p in order:
        hops[2, p].wait_recv()
        pre = landed[2, p].astype(F32) + part[p, me] + bias_ref[...]
        squash = 1.0 / (1.0 + jnp.exp(-pre))
        hidden_ref[:, cols(p)] = (pre * squash).astype(BF16)
        slope = cot_ref[:, cols(p)].astype(F32) * squash * (1.0 + pre * (1.0 - squash))
        slopes[p, me] = slope.astype(BF16)
        hops[3, p] = gather_hop(p, 0)
        hops[3, p].start()
    for s in range(1, 3):
        for p in order:
            hops[2 + s, p].wait_recv()
            hops[3 + s, p] = gather_hop(p, s)
            hops[3 + s, p].start()
    total[...] = jnp.zeros_like(total)
    lanes = (((1,), (1,)), ((), ()))
    for p in order:
        hops[5, p].wait_recv()
        full = slopes[p].reshape(HID, PW)
        direct = jnp.dot(ws_ref[...], full, preferred_element_type=F32)
        back = jnp.dot(wn_ref[...], full, preferred_element_type=F32)
        for k in range(PW // BS):
            b = p * (PW // BS) + k
            part_of = slice(k * BS, (k + 1) * BS)
            direct_ref[b] = direct[:, part_of]
            back_ref[b] = (back[:, part_of] / degree_ref[b : b + 1, :].astype(F32)).astype(BF16)
        total[0] += lax.dot_general(feat_ref[:, cols(p)], full, lanes, preferred_element_type=F32)
        total[1] += lax.dot_general(mean_ref[:, cols(p)], full, lanes, preferred_element_type=F32)
    for k in range(2):
        for c in range(2):
            at = (2 * k + c) * FC
            grads_ref[at : at + FC] = total[k, :, c * BS : (c + 1) * BS]
    for hop in hops.values():
        hop.wait_send()


def dense_call(feat, mean, cot, ws, wn, wst, wnt, bias, degree):
    return pl.pallas_call(
        dense_kernel,
        out_shape=(
            jax.ShapeDtypeStruct((HC, ROWS), BF16),
            jax.ShapeDtypeStruct((NB, FC, BS), BF16),
            jax.ShapeDtypeStruct((NB, FC, BS), F32),
            jax.ShapeDtypeStruct((4 * FC, BS), F32),
        ),
        in_specs=[vmem()] * 9,
        out_specs=(vmem(),) * 4,
        scratch_shapes=[
            pltpu.VMEM((PIECES, NF, HC, PW), F32),
            pltpu.VMEM((3, PIECES, HC, PW), BF16),
            pltpu.VMEM((3, PIECES, HC, PW), BF16),
            pltpu.VMEM((PIECES, NF, HC, PW), BF16),
            pltpu.VMEM((2, FC, HID), F32),
            pltpu.SemaphoreType.DMA((6, PIECES)),
            pltpu.SemaphoreType.DMA((6, PIECES)),
        ],
        compiler_params=pltpu.CompilerParams(collective_id=1, has_side_effects=True, vmem_limit_bytes=48 * MB),
        name="dense_ring",
    )(feat, mean, cot, ws, wn, wst, wnt, bias, degree)


def backward_kernel(plan, vals_hbm, back_ref, direct_ref, home_ref, out_ref, vals, acc, sems):
    loads = load_vals(vals_hbm, vals, sems)
    acc[HALO : HALO + NB] = direct_ref[...]
    acc[:HALO] = jnp.zeros((HALO, FC, BS), F32)
    acc[HALO + NB :] = jnp.zeros((HALO + 1, FC, BS), F32)
    for load in loads:
        load.wait()

    @pl.loop(0, (plan[7, 192] + 2 * GROUP - 1) // (2 * GROUP))
    def _(step):
        for u in range(GROUP):
            slot = step * (2 * GROUP) + 2 * u
            a = jnp.concatenate([vals[plan[3, slot]], vals[plan[3, slot + 1]]], axis=0)
            x = jnp.concatenate([back_ref[plan[4, slot]], back_ref[plan[4, slot + 1]]], axis=1)
            acc[plan[5, slot]] += jnp.dot(x, a, preferred_element_type=F32)

    home_ref[...] = acc[HALO : HALO + NB]
    out_ref[0] = acc[:HALO].astype(BF16)
    out_ref[1] = acc[HALO + NB : EXT].astype(BF16)


def backward_call(plan, vals, back, direct):
    return pl.pallas_call(
        backward_kernel,
        out_shape=(
            jax.ShapeDtypeStruct((NB, FC, BS), F32),
            jax.ShapeDtypeStruct((2, HALO, FC, BS), BF16),
        ),
        in_specs=[smem(), anyspace(), vmem(), vmem()],
        out_specs=(vmem(), vmem()),
        scratch_shapes=[
            pltpu.VMEM((NNZ + 1, BS, BS), BF16),
            pltpu.VMEM((EXT + 1, FC, BS), F32),
            pltpu.SemaphoreType.DMA((8,)),
        ],
        compiler_params=pltpu.CompilerParams(vmem_limit_bytes=48 * MB),
        name="sparse_backward",
    )(plan, vals, back, direct)


SL_A = 4 * FC // 8
SL_B = SL_A // 4


def final_kernel(
    plan, home_ref, out_ref, grads_ref,
    features_ref, self_ref, neigh_ref,
    landed, land_a, sum_a, land_b, sum_b, whole,
    hs, hr, as_, ar, bs, br, cs, cr, ds, dr,
):
    me = lax.axis_index("vtx")
    right, left = lax.rem(me + 1, NV), lax.rem(me + NV - 1, NV)
    core, x, z = lax.rem(me, 2), lax.rem(me // 2, 4), me // 8
    g = 2 * z + core

    def g_peer(k):
        other = lax.rem(g + k, 8)
        return other, {"vtx": ((other // 2) * 4 + x) * 2 + lax.rem(other, 2)}

    def x_peer(k):
        other = lax.rem(x + k, 4)
        return other, {"vtx": (z * 4 + other) * 2 + core}

    greet(
        [{"vtx": left}, {"vtx": right}]
        + [g_peer(k)[1] for k in range(1, 8)]
        + [x_peer(k)[1] for k in range(1, 4)]
    )
    hops = []
    for d, peer in ((0, left), (1, right)):
        for part in range(4):
            hop = pltpu.make_async_remote_copy(
                src_ref=out_ref.at[d, pl.ds(4 * part, 4)], dst_ref=landed.at[d, pl.ds(4 * part, 4)],
                send_sem=hs.at[d, part], recv_sem=hr.at[d, part],
                device_id={"vtx": peer}, device_id_type=MESH,
            )
            hop.start()
            hops.append(hop)

    def exchange(peers, src_of, dst, mine, send, recv):
        trips = []
        for k in range(1, peers + 1):
            other, device = (g_peer if peers == 7 else x_peer)(k)
            trips.append(pltpu.make_async_remote_copy(
                src_ref=src_of(other), dst_ref=dst.at[mine], send_sem=send.at[k - 1], recv_sem=recv.at[k - 1],
                device_id=device, device_id_type=MESH,
            ))
        for trip in trips:
            trip.start()
        return trips

    def rows_a(k):
        return pl.ds(pl.multiple_of(k * SL_A, 8), SL_A)

    def rows_b(k):
        return pl.ds(pl.multiple_of(k * SL_B, 8), SL_B)

    trips = exchange(7, lambda k: grads_ref.at[rows_a(k)], land_a, g, as_, ar)
    for trip in trips:
        trip.wait()
    land_a[g] = grads_ref[rows_a(g)]
    sum_a[...] = jnp.sum(land_a[...], axis=0)
    trips = exchange(3, lambda k: sum_a.at[rows_b(k)], land_b, x, bs, br)
    for trip in trips:
        trip.wait()
    land_b[x] = sum_a[rows_b(x)]
    sum_b[x] = jnp.sum(land_b[...], axis=0) * float(NV * ROWS) ** -0.5
    trips = exchange(3, lambda k: sum_b.at[x], sum_b, x, cs, cr)
    for trip in trips:
        trip.wait()
    whole[g] = sum_b[...].reshape(SL_A, BS)
    trips = exchange(7, lambda k: whole.at[g], whole, g, ds, dr)
    for trip in trips:
        trip.wait()
    every = whole[...].reshape(4 * FC, BS)
    for k, ref in ((0, self_ref), (1, neigh_ref)):
        for c in range(2):
            at = (2 * k + c) * FC
            ref[:, c * BS : (c + 1) * BS] = every[at : at + FC]

    for d in range(2):
        landed[d, HALO] = jnp.zeros((FC, BS), BF16)
    for hop in hops:
        hop.wait()
    for b in range(NB):
        extra = landed[0, plan[6, b]].astype(F32) + landed[1, plan[6, BS + b]].astype(F32)
        features_ref[:, b * BS : (b + 1) * BS] = (home_ref[b] + extra).astype(BF16)


def final_call(plan, home, out, grads):
    dma = pltpu.SemaphoreType.DMA
    return pl.pallas_call(
        final_kernel,
        out_shape=(
            jax.ShapeDtypeStruct((FC, ROWS), BF16),
            jax.ShapeDtypeStruct((FC, HID), F32),
            jax.ShapeDtypeStruct((FC, HID), F32),
        ),
        in_specs=[smem(), vmem(), vmem(), vmem()],
        out_specs=(vmem(), vmem(), vmem()),
        scratch_shapes=[
            pltpu.VMEM((2, HALO + 1, FC, BS), BF16),
            pltpu.VMEM((8, SL_A, BS), F32),
            pltpu.VMEM((SL_A, BS), F32),
            pltpu.VMEM((4, SL_B, BS), F32),
            pltpu.VMEM((4, SL_B, BS), F32),
            pltpu.VMEM((8, SL_A, BS), F32),
            dma((2, 4)), dma((2, 4)), dma((7,)), dma((7,)), dma((3,)), dma((3,)), dma((3,)), dma((3,)), dma((7,)), dma((7,)),
        ],
        compiler_params=pltpu.CompilerParams(collective_id=2, has_side_effects=True, vmem_limit_bytes=48 * MB),
        name="halo_back",
    )(plan, home, out, grads)


def on_device(
    features, w_self, w_neigh, bias_terms, block_vals, block_rows, block_cols, block_count, recv_lists, degree, cotangent
):
    feat, cot = features.T, cotangent.T
    wide = ((0, ENT - NNZ),)
    table = jnp.concatenate(
        [
            jnp.pad(block_rows, wide)[None],
            jnp.pad(block_cols, wide)[None],
            jnp.broadcast_to(block_count, (6, ENT)),
        ],
        axis=0,
    )
    lists = jnp.broadcast_to(jnp.pad(recv_lists, ((0, BS - 2 * HALO),), constant_values=-1)[None], (8, BS))
    degree = degree.reshape(NB, BS)
    halo, plan = halo_call(table, lists, feat)
    mean = forward_call(plan, block_vals, feat, halo, degree)
    hidden, back, direct, grads = dense_call(
        feat, mean, cot, w_self, w_neigh, w_self.T, w_neigh.T, bias_terms.reshape(HC, 1), degree
    )
    home, out = backward_call(plan, block_vals, back, direct)
    grad_features, grad_self, grad_neigh = final_call(plan, home, out, grads)
    return hidden.T, grad_features.T, grad_self, grad_neigh


def solution(mesh):
    placed = (
        P("vtx", "feat"), P("feat", None), P("feat", None), P("feat"), P("vtx", None, None), P("vtx"), P("vtx"), P("vtx"),
        P("vtx"), P("vtx"), P("vtx", "feat"),
    )
    return jax.shard_map(
        on_device,
        mesh=mesh,
        in_specs=placed,
        out_specs=(P("vtx", "feat"), P("vtx", "feat"), P("feat", None), P("feat", None)),
        check_vma=False,
    )
```

time: 484 us -> 130 us (0.27)
  waiting for transfers between devices: 184 us -> 0 us
  local copies, waits for them, and re-layouts: 144 us -> 10.7 us
  Pallas kernels: 0 us -> 118 us
  matrix products: 111 us -> 0 us
  between operations: 15 us -> 1.42 us
  starting transfers between devices: 12.8 us -> 0 us
  other arithmetic: 12.8 us -> 0.07 us
    pallas_call x0 -> x5, Pallas kernels: none -> 118 us  [the longest x1 46.1 us: final_call(): pl.pallas_call(final_kernel, out_shape=(jax.ShapeDtypeStruct((FC, ROWS),...]
    dot_general x12 -> x0, matrix products: 111 us -> none  [the longest x4 52.7 us: add_by_index(): jnp.dot(selector, flat, precision=lax.Precision.HIGHEST, preferred_elemen...]
    psum x1 -> x0, waiting for transfers between devices: 93.4 us -> none  [on_device(): grad_self, grad_neigh = lax.psum((part_self, part_neigh), 'vtx')]
    dot_general x7 -> x0, local copies, waits for them, and re-layouts: 79.4 us -> none  [the longest x1 34.5 us: on_device(): jnp.einsum('nij,njf->nif', weights, operand, preferred_element_type=jnp.f...]
    reduce_scatter x1 -> x0, waiting for transfers between devices: 50.6 us -> none  [on_device(): lax.psum_scatter(partial_pre, 'feat', scatter_dimension=1, tiled=True)]
    all_gather x1 -> x0, waiting for transfers between devices: 30.6 us -> none  [on_device(): slopes_full = lax.all_gather(slopes, 'feat', axis=1, tiled=True)]
    gather x4 -> x0, local copies, waits for them, and re-layouts: 26.6 us -> none  [the longest x1 12.6 us: on_device(): operand = extended[block_cols]]
    slice x6 -> x0, local copies, waits for them, and re-layouts: 12.8 us -> none  [the longest x4 10.6 us: on_device(): home_sum = spread[halo_slots:halo_slots + home_count]]
  transfers between devices with their start and end apart: 7 -> 0, of which waited for: 5 -> 0; matrix products, arithmetic and copies ran while one was open for 7% -> 0% of each run, Pallas kernels for 0% -> 0%
where the time goes in v1:
time: 130 us
  Pallas kernels  118 us (91%)
  local copies, waits for them, and re-layouts  10.7 us (8%)
  between operations  1.42 us (1%)
    pallas_call x1, Pallas kernels, final_call(): pl.pallas_call(final_kernel, out_shape=(jax.ShapeDtypeStruct((FC, ROWS),...  46.1 us
    pallas_call x1, Pallas kernels, dense_call(): pl.pallas_call(dense_kernel, out_shape=(jax.ShapeDtypeStruct((HC, ROWS),...  35.6 us
    pallas_call x1, Pallas kernels, halo_call(): pl.pallas_call(halo_kernel, out_shape=(jax.ShapeDtypeStruct((2, HALO, FC,...  17.7 us
    pallas_call x1, Pallas kernels, backward_call(): pl.pallas_call(backward_kernel, out_shape=(jax.ShapeDtypeStruct((NB, FC,...  10.4 us
    pallas_call x1, Pallas kernels, forward_call(): pl.pallas_call(forward_kernel, out_shape=jax.ShapeDtypeStruct((FC, ROWS),...  7.9 us
    unnamed x20, local copies, waits for them, and re-layouts  7.84 us

profile of v1, /device:TPU:1, one launch (start us, length us, event | category | flops | bytes accessed | tf_op | source)
XLA Modules:
  0.0 129.9 jit_solution(5222225892952381579)
XLA Ops:
  1.3 0.1 pad.16.clone
  1.4 0.7 pad.13
  2.0 0.7 pad.11
  2.7 0.7 pad.12
  3.4 0.1 add_add_fusion.table_ref
  3.5 0.7 copy.17.bias_ref
  4.2 1.0 copy.15
  5.2 1.0 copy.16
  6.2 0.0 copy-start
  6.3 1.4 %copy-done = bf16[4096,192]{0,1:T(8,128)(2,1)S(1)} copy-done((bf16[4096,192]{0,1:T(8,128)(2,1)S(1)}, bf16[4096,192]{0,1:T(8,128)(2,1)}, u32[]{:S(2)}) %copy-start) | copy-done | bytes 1572888
  7.7 17.7 %halo_out.1 = (bf16[2,16,192,128]{3,2,1,0:T(8,128)(2,1)S(1)}, s32[8,384]{1,0:T(8,128)S(1)}) custom-call(s32[8,384]{1,0:T(8,128)S(1)} %add_add_fusion.table_ref, s32[8,128]{1,0:T(8,128)S(1)} %broadcast_in_dim.20.lists_ref, bf16[192,4096]{1,0:T(8,128)(2,1)S(1)} %bitcast.10), custom_call_target="tpu_custom_call" | custom-call | tf_op jit(solution)/shard_map/halo_out/pallas_call | solution.py:137
  25.3 0.0 copy-start.3
  25.4 0.0 copy-start.4
  25.4 0.0 copy-start.5
  25.4 7.9 %sparse_forward.1.mean_ref = bf16[192,4096]{1,0:T(8,128)(2,1)S(1)} custom-call(s32[8,384]{1,0:T(8,128)S(1)} %get-tuple-element.15.plan, bf16[320,128,128]{2,1,0:T(8,128)(2,1)} %vals_hbm.3, bf16[192,4096]{1,0:T(8,128)(2,1)S(1)} %bitcast.11, bf16[2,16,192,128]{3,2,1,0:T(8,128)(2,1)S(1)} %get-tuple-element.16.halo_ref, s32[32,128]{1,0:T(8,128)S(1)} %bitcast.18), custom_call_target="tpu_custom_call" | custom-call | tf_op jit(solution)/shard_map/sparse_forward/pallas_call | solution.py:202
  33.3 0.0 copy-start.2
  33.3 1.1 copy-done.2
  34.4 35.6 %dense_ring.1 = (bf16[64,4096]{1,0:T(8,128)(2,1)S(1)}, bf16[32,192,128]{2,1,0:T(8,128)(2,1)S(1)}, f32[32,192,128]{2,1,0:T(8,128)}, f32[768,128]{1,0:T(8,128)S(1)}) custom-call(bf16[192,4096]{1,0:T(8,128)(2,1)S(1)} %bitcast.12, bf16[192,4096]{1,0:T(8,128)(2,1)} %copy-done.2, bf16[64,4096]{1,0:T(8,128)(2,1)S(1)} %bitcast.17, bf16[192,256]{1,0:T(8,128)(2,1)S(1)} %copy-done.4, ...), custom_call_target="tpu_custom_call" | custom-call | tf_op jit(solution)/shard_map/dense_ring/pallas_call | solution.py:304
  70.1 10.4 %sparse_backward.1 = (f32[32,192,128]{2,1,0:T(8,128)}, bf16[2,16,192,128]{3,2,1,0:T(8,128)(2,1)S(1)}) custom-call(s32[8,384]{1,0:T(8,128)S(1)} %get-tuple-element.15.plan, bf16[320,128,128]{2,1,0:T(8,128)(2,1)} %vals_hbm.3, bf16[32,192,128]{2,1,0:T(8,128)(2,1)S(1)} %get-tuple-element.18.back_ref, f32[32,192,128]{2,1,0:T(8,128)} %get-tuple-element.19.direct_ref), custom_call_target="tpu_custom_call" | custom-call | tf_op jit(solution)/shard_map/sparse_backward/pallas_call | solution.py:350
  80.5 46.1 %halo_back.1 = (bf16[192,4096]{1,0:T(8,128)(2,1)S(1)}, f32[192,256]{1,0:T(8,128)S(1)}, f32[192,256]{1,0:T(8,128)S(1)}) custom-call(s32[8,384]{1,0:T(8,128)S(1)} %get-tuple-element.15.plan, f32[32,192,128]{2,1,0:T(8,128)} %get-tuple-element.20.home_ref, bf16[2,16,192,128]{3,2,1,0:T(8,128)(2,1)S(1)} %get-tuple-element.21.out_ref, ...), custom_call_target="tpu_custom_call" | custom-call | tf_op jit(solution)/shard_map/halo_back/pallas_call | solution.py:459
  126.6 0.8 copy.23
  127.4 1.1 copy.24
  128.6 0.7 copy.25
  129.2 0.7 copy.26
  (11 shorter events, 0.0 us)
Async XLA Ops:
  0.6 24.7 %copy-start.6 = (s32[4096]{0:T(1024)S(1)}, s32[4096]{0:T(1024)}, u32[]{:S(2)}) copy-start(s32[4096]{0:T(1024)} %param.20) | copy-start | bytes 49156
  6.2 1.4 %copy-start = (bf16[4096,192]{0,1:T(8,128)(2,1)S(1)}, bf16[4096,192]{0,1:T(8,128)(2,1)}, u32[]{:S(2)}) copy-start(bf16[4096,192]{0,1:T(8,128)(2,1)} %param.11) | copy-start | bytes 4718596
  7.7 17.7 %copy-start.1 = (bf16[4096,192]{0,1:T(8,128)(2,1)S(1)}, bf16[4096,192]{0,1:T(8,128)(2,1)}, u32[]{:S(2)}) copy-start(bf16[4096,192]{0,1:T(8,128)(2,1)} %param.11) | copy-start | bytes 4718596
  25.3 9.1 %copy-start.3 = (bf16[4096,64]{0,1:T(8,128)(2,1)S(1)}, bf16[4096,64]{0,1:T(8,128)(2,1)}, u32[]{:S(2)}) copy-start(bf16[4096,64]{0,1:T(8,128)(2,1)} %param.21) | copy-start | bytes 1572868
  25.4 9.1 %copy-start.4 = (bf16[192,256]{1,0:T(8,128)(2,1)S(1)}, bf16[192,256]{1,0:T(8,128)(2,1)}, u32[]{:S(2)}) copy-start(bf16[192,256]{1,0:T(8,128)(2,1)} %ws_ref.1) | copy-start | bytes 294916
  25.4 9.1 %copy-start.5 = (bf16[192,256]{1,0:T(8,128)(2,1)S(1)}, bf16[192,256]{1,0:T(8,128)(2,1)}, u32[]{:S(2)}) copy-start(bf16[192,256]{1,0:T(8,128)(2,1)} %wn_ref.1) | copy-start | bytes 294916
  33.3 1.1 copy-start.2

commit v2 on v1

v2 whole, which is shorter than its diff:
```python
import functools

import jax
import jax.numpy as jnp
from jax import lax
from jax.experimental import pallas as pl
from jax.experimental.pallas import tpu as pltpu
from jax.sharding import PartitionSpec as P

MESH = pl.DeviceIdType.MESH
F32, BF16, I32 = jnp.float32, jnp.bfloat16, jnp.int32
BS = 128
NB = 32
HALO = 16
NNZ = 320
EXT = NB + 2 * HALO
FC = 192
HID = 256
HC = 64
ROWS = NB * BS
NV, NF = 32, 4
ENT = 384
PAIRS_F = (NNZ + NB) // 2
PAIRS_B = (NNZ + EXT) // 2
GROUP = 8
PIECES = 8
PW = ROWS // PIECES
MB = 1 << 20


def vmem():
    return pl.BlockSpec(memory_space=pltpu.VMEM)


def smem():
    return pl.BlockSpec(memory_space=pltpu.SMEM)


def anyspace():
    return pl.BlockSpec(memory_space=pl.ANY)


def greet(peers):
    barrier = pltpu.get_barrier_semaphore()
    for peer in peers:
        pl.semaphore_signal(barrier, inc=1, device_id=peer, device_id_type=MESH)
    pl.semaphore_wait(barrier, len(peers))


def iota(shape, dim):
    return lax.broadcasted_iota(I32, shape, dim)


def as_column(row):
    n = row.shape[1]
    diagonal = iota((n, n), 0) == iota((n, n), 1)
    return jnp.sum(jnp.where(diagonal, row, jnp.zeros_like(row)), axis=1, keepdims=True, dtype=row.dtype)


def down(values):
    return jnp.sum(values, axis=0, keepdims=True, dtype=I32)


def pair_schedule(key, other, active, pairs):
    far = 1000
    sub, lane = iota((ENT, ENT), 0), iota((ENT, ENT), 1)
    key = jnp.where(active, key, far)
    key_col = as_column(key)
    rank = down(jnp.where((key_col == key) & (sub < lane), 1, 0))
    group, at = iota((EXT, ENT), 0), iota((EXT, ENT), 1)
    size = jnp.sum(jnp.where(group == key, 1, 0), axis=1, keepdims=True, dtype=I32)
    size = ((size + 1) >> 1) << 1
    start = down(jnp.where(group < key, size, 0))
    slot = jnp.where(active, start + rank, far)
    hit = as_column(slot) == lane

    def at_slots(column, default):
        return down(jnp.where(hit, column - default, 0)) + default

    entry = at_slots(sub[:, :1], NNZ)
    source = at_slots(as_column(other), 0)
    goes_on = jnp.minimum(at_slots(as_column(rank), 1), 1)
    end = down(jnp.where(group <= at, size, 0))
    own = down(jnp.where(group == at, size, 0))
    done = jnp.where(own > 0, (end >> 1) - 1, pairs)
    return [jnp.clip(entry, 0, NNZ), jnp.clip(source, 0, EXT - 1), goes_on, jnp.clip(done, 0, pairs)]


def inverse(lists, first):
    ours = as_column(lists)
    sub, lane = iota((BS, BS), 0), iota((BS, BS), 1)
    hit = (ours == lane) & (sub >= first) & (sub < first + HALO)
    return jnp.clip(down(jnp.where(hit, sub - (first + HALO), 0)) + HALO, 0, HALO)


def load_vals(vals_hbm, vals, sems):
    share = NNZ // 8
    loads = [
        pltpu.make_async_copy(vals_hbm.at[pl.ds(k * share, share)], vals.at[pl.ds(k * share, share)], sems.at[k])
        for k in range(8)
    ]
    for load in loads:
        load.start()
    vals[NNZ] = jnp.zeros((BS, BS), BF16)
    return loads


def sparse_sums(product, goes_on, sums, first, last, carry):
    def step(i, acc):
        for u in range(GROUP):
            t = i * GROUP + u
            acc = acc * goes_on(t).astype(F32) + product(t)
            sums[t] = acc
        return acc

    return lax.fori_loop(first // GROUP, last // GROUP, step, carry)


def gather_kernel(
    rows_ref, cols_ref, count_ref, lists_ref, feat_ref, vals_hbm, degree_ref,
    mean_ref, plan_ref,
    lists_out, lists_in, lists_sm, plan_sm, blocks, sent, halo, vals, sums, sm_sem, ls, lr, bs, br, vs,
):
    me = lax.axis_index("vtx")
    right, left = lax.rem(me + 1, NV), lax.rem(me + NV - 1, NV)
    loads = load_vals(vals_hbm, vals, vs)
    lists_out[...] = jnp.full((8, BS), -1, I32)
    lists_out[0:1, : 2 * HALO] = lists_ref[...]
    greet([{"vtx": left}, {"vtx": right}])
    trips = []
    for k, peer in ((0, right), (1, left)):
        trip = pltpu.make_async_remote_copy(
            src_ref=lists_out, dst_ref=lists_in.at[k], send_sem=ls.at[k], recv_sem=lr.at[k],
            device_id={"vtx": peer}, device_id_type=MESH,
        )
        trip.start()
        trips.append(trip)
    blocks[0] = jnp.zeros((FC, BS), BF16)
    for b in range(NB):
        blocks[1 + b] = feat_ref[:, b * BS : (b + 1) * BS]
    for trip in trips:
        trip.wait()
    local = pltpu.make_async_copy(lists_in, lists_sm, sm_sem)
    local.start()
    local.wait()
    sends = []
    for part in range(4):
        for d in range(2):
            for j in range(4 * part, 4 * part + 4):
                sent[d, j] = blocks[lists_sm[1 - d, 0, j + HALO * d] + 1]
            trip = pltpu.make_async_remote_copy(
                src_ref=sent.at[d, pl.ds(4 * part, 4)], dst_ref=halo.at[pl.ds((HALO + NB) * d + 4 * part, 4)],
                send_sem=bs.at[d, part], recv_sem=br.at[d, part],
                device_id={"vtx": right if d == 0 else left}, device_id_type=MESH,
            )
            trip.start()
            sends.append(trip)

    def wide(ref):
        return jnp.concatenate([ref[...], jnp.zeros((1, ENT - NNZ), I32)], axis=1)

    rows, cols = wide(rows_ref), wide(cols_ref)
    active = iota((1, ENT), 1) < count_ref[0]
    plan = pair_schedule(rows, cols, active, PAIRS_F) + pair_schedule(cols, rows, active, PAIRS_B)
    from_right = inverse(lists_in[1, 0:1], 0)
    from_left = inverse(lists_in[0, 0:1], HALO)
    plan.append(jnp.concatenate([from_right, from_left, jnp.zeros((1, BS), I32)], axis=1))
    for k, row in enumerate(plan):
        plan_ref[k : k + 1] = row
    for k in range(len(plan), 16):
        plan_ref[k : k + 1] = jnp.zeros((1, ENT), I32)
    local = pltpu.make_async_copy(plan_ref, plan_sm, sm_sem)
    local.start()
    local.wait()
    for load in loads:
        load.wait()
    for b in range(NB):
        halo[HALO + b] = blocks[1 + b]
    for trip in sends:
        trip.wait()
    sums[PAIRS_F] = jnp.zeros((FC, BS), F32)

    def product(t):
        a = jnp.concatenate([vals[plan_sm[0, 2 * t]], vals[plan_sm[0, 2 * t + 1]]], axis=1)
        x = jnp.concatenate([halo[plan_sm[1, 2 * t]], halo[plan_sm[1, 2 * t + 1]]], axis=1)
        return lax.dot_general(x, a, (((1,), (1,)), ((), ())), preferred_element_type=F32)

    sparse_sums(product, lambda t: plan_sm[2, 2 * t], sums, 0, PAIRS_F, jnp.zeros((FC, BS), F32))
    for b in range(NB):
        divisor = degree_ref[b : b + 1, :].astype(F32)
        mean_ref[:, b * BS : (b + 1) * BS] = (sums[plan_sm[3, b]] / divisor).astype(BF16)


def gather_call(rows, cols, count, lists, feat, vals, degree):
    dma = pltpu.SemaphoreType.DMA
    return pl.pallas_call(
        gather_kernel,
        out_shape=(jax.ShapeDtypeStruct((FC, ROWS), BF16), jax.ShapeDtypeStruct((16, ENT), I32)),
        in_specs=[vmem(), vmem(), smem(), vmem(), vmem(), anyspace(), vmem()],
        out_specs=(vmem(), vmem()),
        scratch_shapes=[
            pltpu.VMEM((8, BS), I32),
            pltpu.VMEM((2, 8, BS), I32),
            pltpu.SMEM((2, 8, BS), I32),
            pltpu.SMEM((16, ENT), I32),
            pltpu.VMEM((NB + 1, FC, BS), BF16),
            pltpu.VMEM((2, HALO, FC, BS), BF16),
            pltpu.VMEM((EXT, FC, BS), BF16),
            pltpu.VMEM((NNZ + 1, BS, BS), BF16),
            pltpu.VMEM((PAIRS_F + 1, FC, BS), F32),
            dma, dma((2,)), dma((2,)), dma((2, 4)), dma((2, 4)), dma((8,)),
        ],
        compiler_params=pltpu.CompilerParams(collective_id=0, has_side_effects=True, vmem_limit_bytes=48 * MB),
        name="gather_mean",
    )(rows, cols, count, lists, feat, vals, degree)


SL_A = 4 * FC // 8
SL_B = SL_A // 4


def ring_kernel(
    plan, feat_ref, mean_ref, cot_ref, ws_ref, wn_ref, bias_ref, degree_ref, vals_hbm,
    hidden_ref, features_ref, self_ref, neigh_ref,
    wst, wnt, part, staged, landed, slopes, total, vals, sums, back, direct, out, arrived,
    grads, land_a, sum_a, land_b, sum_b, whole,
    send_sem, recv_sem, vs, hs, hr, as_, ar, bs, br, cs, cr, ds, dr,
):
    me = lax.axis_index("feat")
    right, left = lax.rem(me + 1, NF), lax.rem(me + NF - 1, NF)
    v = lax.axis_index("vtx")
    v_right, v_left = lax.rem(v + 1, NV), lax.rem(v + NV - 1, NV)
    core, x, z = lax.rem(v, 2), lax.rem(v // 2, 4), v // 8
    g = 2 * z + core

    def g_peer(k):
        other = lax.rem(g + k, 8)
        return other, {"vtx": ((other // 2) * 4 + x) * 2 + lax.rem(other, 2)}

    def x_peer(k):
        other = lax.rem(x + k, 4)
        return other, {"vtx": (z * 4 + other) * 2 + core}

    loads = load_vals(vals_hbm, vals, vs)
    greet(
        [{"feat": left}, {"feat": right}, {"vtx": v_left}, {"vtx": v_right}]
        + [g_peer(k)[1] for k in range(1, 8)]
        + [x_peer(k)[1] for k in range(1, 4)]
    )

    half = PIECES // 2
    order = [p for k in range(half) for p in (k, half + k)]
    way = {p: (1 if p < half else -1) for p in order}
    peer = {1: right, -1: left}

    def cols(p):
        return slice(p * PW, (p + 1) * PW)

    def chunk(p, back):
        return lax.rem(me - way[p] * back + 2 * NF, NF)

    def reduce_hop(p, s):
        return pltpu.make_async_remote_copy(
            src_ref=staged.at[s, p], dst_ref=landed.at[s, p],
            send_sem=send_sem.at[s, p], recv_sem=recv_sem.at[s, p],
            device_id={"feat": peer[way[p]]}, device_id_type=MESH,
        )

    def gather_hop(p, s):
        owner = chunk(p, s)
        return pltpu.make_async_remote_copy(
            src_ref=slopes.at[p, owner], dst_ref=slopes.at[p, owner],
            send_sem=send_sem.at[3 + s, p], recv_sem=recv_sem.at[3 + s, p],
            device_id={"feat": peer[way[p]]}, device_id_type=MESH,
        )

    wst[...] = ws_ref[...].T
    wnt[...] = wn_ref[...].T
    bias = as_column(bias_ref[...])
    hops = {}
    for p in order:
        pre = jnp.dot(wst[...], feat_ref[:, cols(p)], preferred_element_type=F32)
        pre += jnp.dot(wnt[...], mean_ref[:, cols(p)], preferred_element_type=F32)
        part[p] = pre.reshape(NF, HC, PW)
        staged[0, p] = part[p, chunk(p, 1)].astype(BF16)
        hops[0, p] = reduce_hop(p, 0)
        hops[0, p].start()
    for s in range(1, 3):
        for p in order:
            hops[s - 1, p].wait_recv()
            staged[s, p] = (landed[s - 1, p].astype(F32) + part[p, chunk(p, 1 + s)]).astype(BF16)
            hops[s, p] = reduce_hop(p, s)
            hops[s, p].start()
    for p in order:
        hops[2, p].wait_recv()
        pre = landed[2, p].astype(F32) + part[p, me] + bias
        squash = 1.0 / (1.0 + jnp.exp(-pre))
        hidden_ref[:, cols(p)] = (pre * squash).astype(BF16)
        slope = cot_ref[:, cols(p)].astype(F32) * squash * (1.0 + pre * (1.0 - squash))
        slopes[p, me] = slope.astype(BF16)
        hops[3, p] = gather_hop(p, 0)
        hops[3, p].start()
    for s in range(1, 3):
        for p in order:
            hops[2 + s, p].wait_recv()
            hops[3 + s, p] = gather_hop(p, s)
            hops[3 + s, p].start()
    total[...] = jnp.zeros_like(total)
    lanes = (((1,), (1,)), ((), ()))
    for p in order:
        hops[5, p].wait_recv()
        full = slopes[p].reshape(HID, PW)
        near = jnp.dot(ws_ref[...], full, preferred_element_type=F32)
        far = jnp.dot(wn_ref[...], full, preferred_element_type=F32)
        for k in range(PW // BS):
            b = p * (PW // BS) + k
            part_of = slice(k * BS, (k + 1) * BS)
            direct[b] = near[:, part_of]
            back[b] = (far[:, part_of] / degree_ref[b : b + 1, :].astype(F32)).astype(BF16)
        total[0] += lax.dot_general(feat_ref[:, cols(p)], full, lanes, preferred_element_type=F32)
        total[1] += lax.dot_general(mean_ref[:, cols(p)], full, lanes, preferred_element_type=F32)
    for k in range(2):
        for c in range(2):
            at = (2 * k + c) * FC
            grads[at : at + FC] = total[k, :, c * BS : (c + 1) * BS]

    def exchange(peers, src_of, dst, mine, send, recv):
        trips = []
        for k in range(1, peers + 1):
            other, device = (g_peer if peers == 7 else x_peer)(k)
            trips.append(pltpu.make_async_remote_copy(
                src_ref=src_of(other), dst_ref=dst.at[mine], send_sem=send.at[k - 1], recv_sem=recv.at[k - 1],
                device_id=device, device_id_type=MESH,
            ))
        for trip in trips:
            trip.start()
        return trips

    def rows_a(k):
        return pl.ds(pl.multiple_of(k * SL_A, 8), SL_A)

    def rows_b(k):
        return pl.ds(pl.multiple_of(k * SL_B, 8), SL_B)

    trips = exchange(7, lambda k: grads.at[rows_a(k)], land_a, g, as_, ar)
    for load in loads:
        load.wait()

    def product(t):
        a = jnp.concatenate([vals[plan[4, 2 * t]], vals[plan[4, 2 * t + 1]]], axis=0)
        b = jnp.concatenate([back[plan[5, 2 * t]], back[plan[5, 2 * t + 1]]], axis=1)
        return jnp.dot(b, a, preferred_element_type=F32)

    sums[PAIRS_B] = jnp.zeros((FC, BS), F32)
    sparse_sums(product, lambda t: plan[6, 2 * t], sums, 0, PAIRS_B, jnp.zeros((FC, BS), F32))
    halo_hops = []
    for q in range(4):
        for d, towards in ((0, v_left), (1, v_right)):
            for j in range(4 * q, 4 * q + 4):
                out[d, j] = sums[plan[7, (HALO + NB) * d + j]].astype(BF16)
            hop = pltpu.make_async_remote_copy(
                src_ref=out.at[d, pl.ds(4 * q, 4)], dst_ref=arrived.at[d, pl.ds(4 * q, 4)],
                send_sem=hs.at[d, q], recv_sem=hr.at[d, q],
                device_id={"vtx": towards}, device_id_type=MESH,
            )
            hop.start()
            halo_hops.append(hop)
    for trip in trips:
        trip.wait()
    land_a[g] = grads[rows_a(g)]
    sum_a[...] = jnp.sum(land_a[...], axis=0)
    trips = exchange(3, lambda k: sum_a.at[rows_b(k)], land_b, x, bs, br)
    for b in range(NB):
        direct[b] += sums[plan[7, HALO + b]]
    for d in range(2):
        arrived[d, HALO] = jnp.zeros((FC, BS), BF16)
    for trip in trips:
        trip.wait()
    land_b[x] = sum_a[rows_b(x)]
    sum_b[x] = jnp.sum(land_b[...], axis=0) * float(NV * ROWS) ** -0.5
    trips = exchange(3, lambda k: sum_b.at[x], sum_b, x, cs, cr)
    for trip in trips:
        trip.wait()
    whole[g] = sum_b[...].reshape(SL_A, BS)
    trips = exchange(7, lambda k: whole.at[g], whole, g, ds, dr)
    for hop in halo_hops:
        hop.wait()
    for b in range(NB):
        extra = arrived[0, plan[8, b]].astype(F32) + arrived[1, plan[8, BS + b]].astype(F32)
        features_ref[:, b * BS : (b + 1) * BS] = (direct[b] + extra).astype(BF16)
    for trip in trips:
        trip.wait()
    every = whole[...].reshape(4 * FC, BS)
    for k, ref in ((0, self_ref), (1, neigh_ref)):
        for c in range(2):
            at = (2 * k + c) * FC
            ref[:, c * BS : (c + 1) * BS] = every[at : at + FC]
    for hop in hops.values():
        hop.wait_send()


def ring_call(plan, feat, mean, cot, ws, wn, bias, degree, vals):
    dma = pltpu.SemaphoreType.DMA
    return pl.pallas_call(
        ring_kernel,
        out_shape=(
            jax.ShapeDtypeStruct((HC, ROWS), BF16),
            jax.ShapeDtypeStruct((FC, ROWS), BF16),
            jax.ShapeDtypeStruct((FC, HID), F32),
            jax.ShapeDtypeStruct((FC, HID), F32),
        ),
        in_specs=[smem()] + [vmem()] * 7 + [anyspace()],
        out_specs=(vmem(),) * 4,
        scratch_shapes=[
            pltpu.VMEM((HID, FC), BF16),
            pltpu.VMEM((HID, FC), BF16),
            pltpu.VMEM((PIECES, NF, HC, PW), F32),
            pltpu.VMEM((3, PIECES, HC, PW), BF16),
            pltpu.VMEM((3, PIECES, HC, PW), BF16),
            pltpu.VMEM((PIECES, NF, HC, PW), BF16),
            pltpu.VMEM((2, FC, HID), F32),
            pltpu.VMEM((NNZ + 1, BS, BS), BF16),
            pltpu.VMEM((PAIRS_B + 1, FC, BS), F32),
            pltpu.VMEM((NB, FC, BS), BF16),
            pltpu.VMEM((NB, FC, BS), F32),
            pltpu.VMEM((2, HALO, FC, BS), BF16),
            pltpu.VMEM((2, HALO + 1, FC, BS), BF16),
            pltpu.VMEM((4 * FC, BS), F32),
            pltpu.VMEM((8, SL_A, BS), F32),
            pltpu.VMEM((SL_A, BS), F32),
            pltpu.VMEM((4, SL_B, BS), F32),
            pltpu.VMEM((4, SL_B, BS), F32),
            pltpu.VMEM((8, SL_A, BS), F32),
            dma((6, PIECES)), dma((6, PIECES)), dma((8,)), dma((2, 4)), dma((2, 4)),
            dma((7,)), dma((7,)), dma((3,)), dma((3,)), dma((3,)), dma((3,)), dma((7,)), dma((7,)),
        ],
        compiler_params=pltpu.CompilerParams(collective_id=1, has_side_effects=True, vmem_limit_bytes=60 * MB),
        name="ring_and_back",
    )(plan, feat, mean, cot, ws, wn, bias, degree, vals)


def on_device(
    features, w_self, w_neigh, bias_terms, block_vals, block_rows, block_cols, block_count, recv_lists, degree, cotangent
):
    feat, cot = features.T, cotangent.T
    degree = degree.reshape(NB, BS)
    mean, plan = gather_call(
        block_rows.reshape(1, NNZ), block_cols.reshape(1, NNZ), block_count, recv_lists.reshape(1, 2 * HALO),
        feat, block_vals, degree,
    )
    hidden, grad_features, grad_self, grad_neigh = ring_call(
        plan, feat, mean, cot, w_self, w_neigh, bias_terms.reshape(1, HC), degree, block_vals
    )
    return hidden.T, grad_features.T, grad_self, grad_neigh


def solution(mesh):
    placed = (
        P("vtx", "feat"), P("feat", None), P("feat", None), P("feat"), P("vtx", None, None), P("vtx"), P("vtx"), P("vtx"),
        P("vtx"), P("vtx"), P("vtx", "feat"),
    )
    return jax.shard_map(
        on_device,
        mesh=mesh,
        in_specs=placed,
        out_specs=(P("vtx", "feat"), P("vtx", "feat"), P("feat", None), P("feat", None)),
        check_vma=False,
    )
```

time: 130 us -> 121 us (0.931)
  Pallas kernels: 118 us -> 107 us
    pallas_call x5 -> x2, Pallas kernels: 118 us -> 107 us  [the longest x1 80.9 us: ring_call(): pl.pallas_call(ring_kernel, out_shape=(jax.ShapeDtypeStruct((HC, ROWS), B...]
    unnamed x20 -> x18, local copies, waits for them, and re-layouts: 7.84 us -> 10.5 us
    pad x3 -> x0, local copies, waits for them, and re-layouts: 2.03 us -> none  [the longest x1 0.68 us: on_device(): jnp.pad(block_cols, wide)[None]]
where the time goes in v2:
time: 121 us
  Pallas kernels  107 us (88%)
  local copies, waits for them, and re-layouts  11.9 us (10%)
  between operations  1.31 us (1%)
    pallas_call x1, Pallas kernels, ring_call(): pl.pallas_call(ring_kernel, out_shape=(jax.ShapeDtypeStruct((HC, ROWS), B...  80.9 us
    pallas_call x1, Pallas kernels, gather_call(): pl.pallas_call(gather_kernel, out_shape=(jax.ShapeDtypeStruct((FC, ROWS),...  26.4 us
    unnamed x18, local copies, waits for them, and re-layouts  10.5 us

profile of v2, /device:TPU:1, one launch (start us, length us, event | category | flops | bytes accessed | tf_op | source)
XLA Modules:
  0.0 120.5 jit_solution(8048737452781236494)
XLA Ops:
  1.3 0.7 reshape.23.rows_ref
  2.0 0.7 reshape.24.cols_ref
  2.6 0.0 copy-start
  2.6 1.4 %copy-done = bf16[4096,192]{0,1:T(8,128)(2,1)S(1)} copy-done((bf16[4096,192]{0,1:T(8,128)(2,1)S(1)}, bf16[4096,192]{0,1:T(8,128)(2,1)}, u32[]{:S(2)}) %copy-start) | copy-done | bytes 1572888
  4.1 0.0 copy-start.2
  4.1 0.7 copy-done.2
  4.8 0.0 copy-start.4
  4.8 0.7 copy-done.4
  5.4 26.4 %gather_mean.1 = (bf16[192,4096]{1,0:T(8,128)(2,1)S(1)}, s32[16,384]{1,0:T(8,128)S(1)}) custom-call(s32[1,320]{1,0:T(1,128)S(1)} %reshape.23.rows_ref, s32[1,320]{1,0:T(1,128)S(1)} %reshape.24.cols_ref, s32[1]{0:T(128)S(6)} %copy.19.count_ref, s32[1,32]{1,0:T(1,128)S(1)} %bitcast.11, bf16[192,4096]{1,0:T(8,128)(2,1)S(1)} %bitcast.8, ...), custom_call_target="tpu_custom_call" | custom-call | tf_op jit(solution)/shard_map/gather_mean/pallas_call | solution.py:196
  31.9 0.0 copy-start.1
  31.9 1.1 copy-done.1
  33.0 0.0 copy-start.3
  33.0 0.6 copy-done.3
  33.6 80.9 %ring_and_back.1 = (bf16[64,4096]{1,0:T(8,128)(2,1)}, bf16[192,4096]{1,0:T(8,128)(2,1)}, f32[192,256]{1,0:T(8,128)}, f32[192,256]{1,0:T(8,128)}) custom-call(s32[16,384]{1,0:T(8,128)} %copy-done.3, bf16[192,4096]{1,0:T(8,128)(2,1)} %bitcast.7, bf16[192,4096]{1,0:T(8,128)(2,1)} %copy-done.1, bf16[64,4096]{1,0:T(8,128)(2,1)} %bitcast.14, ...), custom_call_target="tpu_custom_call" | custom-call | tf_op jit(solution)/shard_map/ring_and_back/pallas_call | solution.py:404
  114.5 1.9 %copy.20 = bf16[4096,64]{0,1:T(8,128)(2,1)} copy(bf16[4096,64]{0,1:T(8,128)(2,1)} %bitcast.13) | data formatting | bytes 1048576
  116.4 0.0 copy-start.6
  116.4 0.0 copy-start.5
  116.4 2.8 %copy.21 = bf16[4096,192]{0,1:T(8,128)(2,1)} copy(bf16[4096,192]{0,1:T(8,128)(2,1)} %bitcast.12) | data formatting | bytes 3145728
  119.2 0.0 copy-done.6
  119.2 0.7 copy.22
  119.9 0.0 copy-done.5
  119.9 0.7 copy.23
Async XLA Ops:
  2.6 1.4 %copy-start = (bf16[4096,192]{0,1:T(8,128)(2,1)S(1)}, bf16[4096,192]{0,1:T(8,128)(2,1)}, u32[]{:S(2)}) copy-start(bf16[4096,192]{0,1:T(8,128)(2,1)} %param.11) | copy-start | bytes 4718596
  4.1 0.7 copy-start.2
  4.8 0.7 copy-start.4
  31.9 1.1 copy-start.1
  33.0 0.6 copy-start.3
  116.4 2.8 %copy-start.6 = (f32[192,256]{1,0:T(8,128)S(1)}, f32[192,256]{1,0:T(8,128)}, u32[]{:S(2)}) copy-start(f32[192,256]{1,0:T(8,128)} %get-tuple-element.22) | copy-start | bytes 589828
  116.4 3.4 %copy-start.5 = (f32[192,256]{1,0:T(8,128)S(1)}, f32[192,256]{1,0:T(8,128)}, u32[]{:S(2)}) copy-start(f32[192,256]{1,0:T(8,128)} %get-tuple-element.23) | copy-start | bytes 589828

commit v3 on v2

v3 whole, which is shorter than its diff:
```python
import functools

import jax
import jax.numpy as jnp
from jax import lax
from jax.experimental import pallas as pl
from jax.experimental.pallas import tpu as pltpu
from jax.sharding import PartitionSpec as P

MESH = pl.DeviceIdType.MESH
F32, BF16, I32 = jnp.float32, jnp.bfloat16, jnp.int32
BS = 128
NB = 32
HALO = 16
NNZ = 320
EXT = NB + 2 * HALO
FC = 192
HID = 256
HC = 64
ROWS = NB * BS
NV, NF = 32, 4
ENT = 384
PIECES = 8
PB = NB // PIECES
PAIRS_F = (NNZ + NB) // 2
PAIRS_B = (NNZ + EXT) // 2
PIECE_PAIRS = PAIRS_F // PIECES
GROUP = 24
ZERO = NB
SL_A = 4 * FC // 8
SL_B = SL_A // 4
MB = 1 << 20


def vmem():
    return pl.BlockSpec(memory_space=pltpu.VMEM)


def smem():
    return pl.BlockSpec(memory_space=pltpu.SMEM)


def anyspace():
    return pl.BlockSpec(memory_space=pl.ANY)


def greet(peers):
    barrier = pltpu.get_barrier_semaphore()
    for peer in peers:
        pl.semaphore_signal(barrier, inc=1, device_id=peer, device_id_type=MESH)
    pl.semaphore_wait(barrier, len(peers))


def iota(shape, dim):
    return lax.broadcasted_iota(I32, shape, dim)


def as_column(row):
    n = row.shape[1]
    diagonal = iota((n, n), 0) == iota((n, n), 1)
    return jnp.sum(jnp.where(diagonal, row, jnp.zeros_like(row)), axis=1, keepdims=True, dtype=row.dtype)


def down(values):
    return jnp.sum(values, axis=0, keepdims=True, dtype=I32)


def group_sizes(key):
    size = jnp.sum(jnp.where(iota((EXT, ENT), 0) == key, 1, 0), axis=1, keepdims=True, dtype=I32)
    return ((size + 1) >> 1) << 1


def order_groups(key):
    block, lane = iota((EXT, ENT), 0), iota((EXT, ENT), 1)
    size = group_sizes(key)
    size_row = down(jnp.where(block == lane, size, 0))
    earlier = (size < size_row) | ((size == size_row) & (block < lane))
    place = down(jnp.where(earlier & (block < NB), 1, 0))
    place_col = as_column(place)[:EXT]
    at_place = down(jnp.where((place_col == lane) & (block < NB), block, 0))
    of_entry = down(jnp.where(block == key, place_col, 0))
    return place, at_place, of_entry


def pair_schedule(key, other, active):
    far = 1000
    sub, lane = iota((ENT, ENT), 0), iota((ENT, ENT), 1)
    key = jnp.where(active, key, far)
    key_col = as_column(key)
    rank = down(jnp.where((key_col == key) & (sub < lane), 1, 0))
    group, at = iota((EXT, ENT), 0), iota((EXT, ENT), 1)
    size = group_sizes(key)
    start = down(jnp.where(group < key, size, 0))
    slot = jnp.where(active, start + rank, far)
    hit = as_column(slot) == lane

    def at_slots(column, default):
        return down(jnp.where(hit, column - default, 0)) + default

    entry = at_slots(sub[:, :1], NNZ)
    source = at_slots(as_column(other), 0)
    goes_on = jnp.minimum(at_slots(as_column(rank), 1), 1)
    end = down(jnp.where(group <= at, size, 0))
    own = down(jnp.where(group == at, size, 0))
    done = jnp.where(own > 0, (end >> 1) - 1, PAIRS_B)
    return [jnp.clip(entry, 0, NNZ), jnp.clip(source, 0, EXT), goes_on, jnp.clip(done, 0, PAIRS_B)]


def inverse(lists, first):
    ours = as_column(lists)
    sub, lane = iota((BS, BS), 0), iota((BS, BS), 1)
    hit = (ours == lane) & (sub >= first) & (sub < first + HALO)
    return jnp.clip(down(jnp.where(hit, sub - (first + HALO), 0)) + HALO, 0, HALO)


def layer_kernel(
    rows_hbm, cols_hbm, count_ref, lists_hbm, feat_hbm, cot_hbm, degree_hbm, ws_ref, wn_ref, bias_hbm, vals_hbm,
    hidden_hbm, base_hbm, arrived, grads_hbm, plan_hbm,
    rows_v, cols_v, lists_v, bias_v, degree_v, rdeg, lists_out, lists_in, lists_sm, plan_v, plan,
    ext, landed_halo, cot, vals, sums, sent, mean, wst, wnt, part, staged, landed, slopes, hid, back, base, hidden,
    total, grads, land_a, sum_a, land_b, sum_b, whole,
    small_sem, feat_sem, cot_sem, vals_sem, sm_sem, ls, lr, hs, hr,
    send_sem, recv_sem, bs, br, as_, ar, zs, zr, cs, cr, ds, dr, out_sem,
):
    me = lax.axis_index("feat")
    right, left = lax.rem(me + 1, NF), lax.rem(me + NF - 1, NF)
    v = lax.axis_index("vtx")
    v_right, v_left = lax.rem(v + 1, NV), lax.rem(v + NV - 1, NV)
    h, z = lax.rem(v, 8), v // 8

    def h_peer(k):
        other = lax.rem(h + k, 8)
        return other, {"vtx": z * 8 + other}

    def z_peer(k):
        other = lax.rem(z + k, 4)
        return other, {"vtx": other * 8 + h}

    small = [
        pltpu.make_async_copy(src, dst, small_sem.at[k])
        for k, (src, dst) in enumerate(
            [(lists_hbm, lists_v), (rows_hbm, rows_v), (cols_hbm, cols_v), (bias_hbm, bias_v), (degree_hbm, degree_v)]
        )
    ]
    feat_loads = [
        pltpu.make_async_copy(feat_hbm.at[:, pl.ds(b * BS, BS)], ext.at[b], feat_sem.at[b]) for b in range(NB)
    ]
    cot_loads = [
        pltpu.make_async_copy(cot_hbm.at[:, pl.ds(b * BS, BS)], cot.at[b], cot_sem.at[b]) for b in range(NB)
    ]
    share = NNZ // 8
    val_loads = [
        pltpu.make_async_copy(vals_hbm.at[pl.ds(k * share, share)], vals.at[pl.ds(k * share, share)], vals_sem.at[k])
        for k in range(8)
    ]
    for load in small + feat_loads:
        load.start()
    barrier = pltpu.get_barrier_semaphore()
    peers = (
        [{"vtx": v_left}, {"vtx": v_right}, {"feat": left}, {"feat": right}]
        + [h_peer(k)[1] for k in range(1, 8)]
        + [z_peer(k)[1] for k in range(1, 4)]
    )
    for peer in peers:
        pl.semaphore_signal(barrier, inc=1, device_id=peer, device_id_type=MESH)
    for load in val_loads + cot_loads:
        load.start()
    small[0].wait()
    lists_out[...] = jnp.full((8, BS), -1, I32)
    lists_out[0:1, : 2 * HALO] = lists_v[...].reshape(1, 2 * HALO)
    ext[ZERO] = jnp.zeros((FC, BS), BF16)
    vals[NNZ] = jnp.zeros((BS, BS), BF16)
    sums[PAIRS_B] = jnp.zeros((FC, BS), F32)
    pl.semaphore_wait(barrier, len(peers))

    trips = []
    for k, peer in ((0, v_right), (1, v_left)):
        trip = pltpu.make_async_remote_copy(
            src_ref=lists_out, dst_ref=lists_in.at[k], send_sem=ls.at[k], recv_sem=lr.at[k],
            device_id={"vtx": peer}, device_id_type=MESH,
        )
        trip.start()
        trips.append(trip)
    for load in small[1:] + feat_loads:
        load.wait()
    wst[...] = ws_ref[...].T
    wnt[...] = wn_ref[...].T
    bias = as_column(bias_v[...].reshape(1, HC))
    for b in range(NB):
        rdeg[b] = jnp.broadcast_to(1.0 / degree_v[b : b + 1, :].astype(F32), (8, BS))
    for trip in trips:
        trip.wait()
    local = pltpu.make_async_copy(lists_in, lists_sm, sm_sem)
    local.start()
    local.wait()
    halo_trips = []
    for q in range(4):
        for d in range(2):
            for j in range(4 * q, 4 * q + 4):
                sent[d, j] = ext[lax.rem(lists_sm[1 - d, 0, j + HALO * d] + NB + 1, NB + 1)]
            trip = pltpu.make_async_remote_copy(
                src_ref=sent.at[d, pl.ds(4 * q, 4)], dst_ref=landed_halo.at[d, pl.ds(4 * q, 4)],
                send_sem=hs.at[d, q], recv_sem=hr.at[d, q],
                device_id={"vtx": v_right if d == 0 else v_left}, device_id_type=MESH,
            )
            trip.start()
            halo_trips.append(trip)

    def wide(ref):
        return jnp.concatenate([ref[...].reshape(1, NNZ), jnp.zeros((1, ENT - NNZ), I32)], axis=1)

    rows, cols = wide(rows_v), wide(cols_v)
    active = iota((1, ENT), 1) < count_ref[0]
    where_col = jnp.where(cols < HALO, cols + NB + 1, jnp.where(cols < HALO + NB, cols - HALO, cols + 1))
    place, at_place, entry_place = order_groups(jnp.where(active, rows, 1000))
    table = pair_schedule(entry_place, where_col, active) + pair_schedule(cols, entry_place, active)
    from_right = inverse(lists_in[1, 0:1], 0)
    from_left = inverse(lists_in[0, 0:1], HALO)
    table.append(jnp.concatenate([from_right, from_left, jnp.zeros((1, BS), I32)], axis=1))
    table += [jnp.clip(place, 0, NB - 1), jnp.clip(at_place, 0, NB - 1)]
    for k, row in enumerate(table):
        plan_v[k : k + 1] = row
    for k in range(len(table), 16):
        plan_v[k : k + 1] = jnp.zeros((1, ENT), I32)
    local = pltpu.make_async_copy(plan_v, plan, sm_sem)
    local.start()
    plan_out = pltpu.make_async_copy(plan_v, plan_hbm, out_sem.at[0])
    plan_out.start()
    local.wait()

    def block_at(q):
        return plan[10, q]

    def side_by_side(blocks):
        return jnp.concatenate(blocks, axis=1)

    for p in range(PIECES):
        own = side_by_side([ext[block_at(p * PB + k)] for k in range(PB)])
        pre = jnp.dot(wst[...], own, preferred_element_type=F32)
        for k in range(PB):
            part[p * PB + k] = pre[:, k * BS : (k + 1) * BS]
    for load in val_loads + cot_loads:
        load.wait()
    for trip in halo_trips:
        trip.wait()
    for d in range(2):
        for j in range(HALO):
            ext[NB + 1 + HALO * d + j] = landed_halo[d, j]

    way = {p: 1 - 2 * (p % 2) for p in range(PIECES)}
    peer_of = {1: right, -1: left}

    def chunk(w, back_by):
        return lax.rem(me - w * back_by + 2 * NF, NF)

    def reduce_hop(p, s, w):
        return pltpu.make_async_remote_copy(
            src_ref=staged.at[s, p], dst_ref=landed.at[s, p],
            send_sem=send_sem.at[s, p], recv_sem=recv_sem.at[s, p],
            device_id={"feat": peer_of[w]}, device_id_type=MESH,
        )

    def gather_hop(p, s, w):
        owner = chunk(w, s)
        return pltpu.make_async_remote_copy(
            src_ref=slopes.at[p, owner], dst_ref=slopes.at[p, owner],
            send_sem=send_sem.at[3 + s, p], recv_sem=recv_sem.at[3 + s, p],
            device_id={"feat": peer_of[w]}, device_id_type=MESH,
        )

    def chunk_rows(c):
        return pl.ds(pl.multiple_of(c * HC, HC), HC)

    def forward_product(t):
        a = side_by_side([vals[plan[0, 2 * t]], vals[plan[0, 2 * t + 1]]])
        x = side_by_side([ext[plan[1, 2 * t]], ext[plan[1, 2 * t + 1]]])
        return lax.dot_general(x, a, (((1,), (1,)), ((), ())), preferred_element_type=F32)

    def reduce_on(p, s, w):
        reduce_hop(p, s - 1, w).wait_recv()
        for k in range(PB):
            more = part[p * PB + k, chunk_rows(chunk(w, 1 + s))]
            staged[s, p, k] = (landed[s - 1, p, k].astype(F32) + more).astype(BF16)
        reduce_hop(p, s, w).start()

    def forward_pieces(i, acc):
        for w in (1, -1):
            p = 2 * i + (0 if w == 1 else 1)
            for u in range(PIECE_PAIRS):
                t = p * PIECE_PAIRS + u
                acc = acc * plan[2, 2 * t].astype(F32) + forward_product(t)
                sums[t] = acc
            for k in range(PB):
                q = p * PB + k
                scale = rdeg[block_at(q)][0:1]
                mean[q] = (sums[plan[3, q]] * scale).astype(BF16)
            pre = jnp.dot(wnt[...], side_by_side([mean[p * PB + k] for k in range(PB)]), preferred_element_type=F32)
            for k in range(PB):
                q = p * PB + k
                part[q] = part[q] + pre[:, k * BS : (k + 1) * BS]
                staged[0, p, k] = part[q, chunk_rows(chunk(w, 1))].astype(BF16)
            reduce_hop(p, 0, w).start()
        return acc

    acc = forward_pieces(0, jnp.zeros((FC, BS), F32))

    def forward_step(i, acc):
        acc = forward_pieces(i, acc)
        for w in (1, -1):
            reduce_on(2 * i - 2 + (0 if w == 1 else 1), 1, w)
        return acc

    lax.fori_loop(1, PIECES // 2, forward_step, acc)
    for p in (PIECES - 2, PIECES - 1):
        reduce_on(p, 1, way[p])
    for p in range(PIECES):
        reduce_on(p, 2, way[p])
    for p in range(PIECES):
        reduce_hop(p, 2, way[p]).wait_recv()
        for k in range(PB):
            q = p * PB + k
            pre = landed[2, p, k].astype(F32) + part[q, chunk_rows(me)] + bias
            squash = 1.0 / (1.0 + jnp.exp(-pre))
            hid[q] = (pre * squash).astype(BF16)
            slope = cot[block_at(q)].astype(F32) * squash * (1.0 + pre * (1.0 - squash))
            slopes[p, me, k] = slope.astype(BF16)
        gather_hop(p, 0, way[p]).start()
    for s in range(1, 3):
        for p in range(PIECES):
            gather_hop(p, s - 1, way[p]).wait_recv()
            gather_hop(p, s, way[p]).start()
    total[...] = jnp.zeros_like(total)
    lanes = (((1,), (1,)), ((), ()))

    def slopes_of(p):
        return side_by_side([slopes[p, :, k].reshape(HID, BS) for k in range(PB)])

    for p in range(PIECES):
        gather_hop(p, 2, way[p]).wait_recv()
        full = slopes_of(p)
        far = jnp.dot(wn_ref[...], full, preferred_element_type=F32)
        for k in range(PB):
            q = p * PB + k
            back[q] = (far[:, k * BS : (k + 1) * BS] * rdeg[block_at(q)][0:1]).astype(BF16)
        own = side_by_side([ext[block_at(p * PB + k)] for k in range(PB)])
        near = side_by_side([mean[p * PB + k] for k in range(PB)])
        total[0] += lax.dot_general(own, full, lanes, preferred_element_type=F32)
        total[1] += lax.dot_general(near, full, lanes, preferred_element_type=F32)
    for k in range(2):
        for c in range(2):
            at = (2 * k + c) * FC
            grads[at : at + FC] = total[k, :, c * BS : (c + 1) * BS].astype(BF16)

    def exchange(peer_at, count, src_of, dst, mine, send, recv):
        trips = []
        for k in range(1, count + 1):
            other, device = peer_at(k)
            trips.append(pltpu.make_async_remote_copy(
                src_ref=src_of(other), dst_ref=dst.at[mine], send_sem=send.at[k - 1], recv_sem=recv.at[k - 1],
                device_id=device, device_id_type=MESH,
            ))
        for trip in trips:
            trip.start()
        return trips

    def rows_a(k):
        return pl.ds(pl.multiple_of(k * SL_A, 32), SL_A)

    def rows_b(k):
        return pl.ds(pl.multiple_of(k * SL_B, 8), SL_B)

    trips = exchange(h_peer, 7, lambda k: grads.at[rows_a(k)], land_a, h, as_, ar)

    def backward_product(t):
        a = jnp.concatenate([vals[plan[4, 2 * t]], vals[plan[4, 2 * t + 1]]], axis=0)
        b = side_by_side([back[plan[5, 2 * t]], back[plan[5, 2 * t + 1]]])
        return jnp.dot(b, a, preferred_element_type=F32)

    def backward_step(i, acc):
        for u in range(GROUP):
            t = i * GROUP + u
            acc = acc * plan[6, 2 * t].astype(F32) + backward_product(t)
            sums[t] = acc
        return acc

    lax.fori_loop(0, PAIRS_B // GROUP, backward_step, jnp.zeros((FC, BS), F32))
    back_trips = []
    for q in range(4):
        for d, towards in ((0, v_left), (1, v_right)):
            for j in range(4 * q, 4 * q + 4):
                sent[d, j] = sums[plan[7, (HALO + NB) * d + j]].astype(BF16)
            trip = pltpu.make_async_remote_copy(
                src_ref=sent.at[d, pl.ds(4 * q, 4)], dst_ref=arrived.at[d, pl.ds(4 * q, 4)],
                send_sem=bs.at[d, q], recv_sem=br.at[d, q],
                device_id={"vtx": towards}, device_id_type=MESH,
            )
            trip.start()
            back_trips.append(trip)
    for trip in trips:
        trip.wait()
    land_a[h] = grads[rows_a(h)]
    sum_a[...] = jnp.sum(land_a[...].astype(F32), axis=0)
    trips = exchange(z_peer, 3, lambda k: sum_a.at[rows_b(k)], land_b, z, zs, zr)
    for b in range(NB):
        hidden[:, b * BS : (b + 1) * BS] = hid[plan[9, b]]
    outs = [plan_out, pltpu.make_async_copy(hidden, hidden_hbm, out_sem.at[1])]
    outs[1].start()
    for trip in trips:
        trip.wait()
    land_b[z] = sum_a[rows_b(z)]
    sum_b[z] = jnp.sum(land_b[...], axis=0) * float(NV * ROWS) ** -0.5
    trips = exchange(z_peer, 3, lambda k: sum_b.at[z], sum_b, z, cs, cr)
    for p in range(PIECES):
        near = jnp.dot(ws_ref[...], slopes_of(p), preferred_element_type=F32)
        for k in range(PB):
            part[p * PB + k, :FC] = near[:, k * BS : (k + 1) * BS]
    for trip in trips:
        trip.wait()
    whole[h] = sum_b[...].reshape(SL_A, BS)
    trips = exchange(h_peer, 7, lambda k: whole.at[h], whole, h, ds, dr)
    for c in range(4):
        for b in range(8 * c, 8 * c + 8):
            base[b] = part[plan[9, b], :FC] + sums[plan[7, HALO + b]]
        outs.append(pltpu.make_async_copy(base.at[pl.ds(8 * c, 8)], base_hbm.at[pl.ds(8 * c, 8)], out_sem.at[2 + c]))
        outs[-1].start()
    for trip in trips:
        trip.wait()
    outs.append(pltpu.make_async_copy(whole, grads_hbm, out_sem.at[6]))
    outs[-1].start()
    for trip in back_trips:
        trip.wait()
    for s in range(3):
        for p in range(PIECES):
            reduce_hop(p, s, way[p]).wait_send()
            gather_hop(p, s, way[p]).wait_send()
    for out in outs:
        out.wait()


def layer_call(rows, cols, count, lists, feat, cot, degree, ws, wn, bias, vals):
    dma = pltpu.SemaphoreType.DMA
    V = pltpu.VMEM
    return pl.pallas_call(
        layer_kernel,
        out_shape=(
            jax.ShapeDtypeStruct((HC, ROWS), BF16),
            jax.ShapeDtypeStruct((NB, FC, BS), F32),
            jax.ShapeDtypeStruct((2, HALO, FC, BS), BF16),
            jax.ShapeDtypeStruct((8, SL_A, BS), F32),
            jax.ShapeDtypeStruct((16, ENT), I32),
        ),
        in_specs=[anyspace(), anyspace(), smem()] + [anyspace()] * 4 + [vmem()] * 2 + [anyspace()] * 2,
        out_specs=(anyspace(),) * 5,
        scratch_shapes=[
            V((NNZ,), I32),
            V((NNZ,), I32),
            V((2 * HALO,), I32),
            V((HC,), F32),
            V((NB, BS), I32),
            V((NB, 8, BS), F32),
            V((8, BS), I32),
            V((2, 8, BS), I32),
            pltpu.SMEM((2, 8, BS), I32),
            V((16, ENT), I32),
            pltpu.SMEM((16, ENT), I32),
            V((EXT + 1, FC, BS), BF16),
            V((2, HALO, FC, BS), BF16),
            V((NB, HC, BS), BF16),
            V((NNZ + 1, BS, BS), BF16),
            V((PAIRS_B + 1, FC, BS), F32),
            V((2, HALO, FC, BS), BF16),
            V((NB, FC, BS), BF16),
            V((HID, FC), BF16),
            V((HID, FC), BF16),
            V((NB, HID, BS), F32),
            V((3, PIECES, PB, HC, BS), BF16),
            V((3, PIECES, PB, HC, BS), BF16),
            V((PIECES, NF, PB, HC, BS), BF16),
            V((NB, HC, BS), BF16),
            V((NB, FC, BS), BF16),
            V((NB, FC, BS), F32),
            V((HC, ROWS), BF16),
            V((2, FC, HID), F32),
            V((4 * FC, BS), BF16),
            V((8, SL_A, BS), BF16),
            V((SL_A, BS), F32),
            V((4, SL_B, BS), F32),
            V((4, SL_B, BS), F32),
            V((8, SL_A, BS), F32),
            dma((5,)), dma((NB,)), dma((NB,)), dma((8,)), dma, dma((2,)), dma((2,)), dma((2, 4)), dma((2, 4)),
            dma((6, PIECES)), dma((6, PIECES)), dma((2, 4)), dma((2, 4)),
            dma((7,)), dma((7,)), dma((3,)), dma((3,)), dma((3,)), dma((3,)), dma((7,)), dma((7,)), dma((7,)),
        ],
        compiler_params=pltpu.CompilerParams(collective_id=0, has_side_effects=True, vmem_limit_bytes=60 * MB),
        name="layer",
    )(rows, cols, count, lists, feat, cot, degree, ws, wn, bias, vals)


def results_kernel(
    plan_hbm, base_hbm, arrived_hbm, hidden_in, grads_hbm,
    hidden_out, features_hbm, self_ref, neigh_ref,
    plan, base, arrived, features, grads, sems,
):
    loads = [pltpu.make_async_copy(plan_hbm, plan, sems.at[0]), pltpu.make_async_copy(grads_hbm, grads, sems.at[1])]
    loads += [pltpu.make_async_copy(arrived_hbm.at[d], arrived.at[d, pl.ds(0, HALO)], sems.at[2 + d]) for d in range(2)]
    pieces = [
        pltpu.make_async_copy(base_hbm.at[pl.ds(8 * c, 8)], base.at[pl.ds(8 * c, 8)], sems.at[4 + c]) for c in range(4)
    ]
    copy = pltpu.make_async_copy(hidden_in, hidden_out, sems.at[8])
    for load in loads + pieces + [copy]:
        load.start()
    for d in range(2):
        arrived[d, HALO] = jnp.zeros((FC, BS), BF16)
    for load in loads:
        load.wait()
    outs = []
    for c in range(4):
        pieces[c].wait()
        for b in range(8 * c, 8 * c + 8):
            extra = arrived[0, plan[8, b]].astype(F32) + arrived[1, plan[8, BS + b]].astype(F32)
            features[:, b * BS : (b + 1) * BS] = (base[b] + extra).astype(BF16)
        at = pl.ds(8 * c * BS, 8 * BS)
        outs.append(pltpu.make_async_copy(features.at[:, at], features_hbm.at[:, at], sems.at[9 + c]))
        outs[-1].start()
    every = grads[...].reshape(4 * FC, BS)
    for k, ref in ((0, self_ref), (1, neigh_ref)):
        for c in range(2):
            at = (2 * k + c) * FC
            ref[:, c * BS : (c + 1) * BS] = every[at : at + FC]
    for out in outs + [copy]:
        out.wait()


def results_call(plan, base, arrived, hidden, grads):
    V = pltpu.VMEM
    return pl.pallas_call(
        results_kernel,
        out_shape=(
            jax.ShapeDtypeStruct((HC, ROWS), BF16),
            jax.ShapeDtypeStruct((FC, ROWS), BF16),
            jax.ShapeDtypeStruct((FC, HID), F32),
            jax.ShapeDtypeStruct((FC, HID), F32),
        ),
        in_specs=[anyspace()] * 5,
        out_specs=(anyspace(), anyspace(), vmem(), vmem()),
        scratch_shapes=[
            pltpu.SMEM((16, ENT), I32),
            V((NB, FC, BS), F32),
            V((2, HALO + 1, FC, BS), BF16),
            V((FC, ROWS), BF16),
            V((8, SL_A, BS), F32),
            pltpu.SemaphoreType.DMA((13,)),
        ],
        compiler_params=pltpu.CompilerParams(vmem_limit_bytes=48 * MB),
        name="results",
    )(plan, base, arrived, hidden, grads)


def on_device(
    features, w_self, w_neigh, bias_terms, block_vals, block_rows, block_cols, block_count, recv_lists, degree, cotangent
):
    hidden, base, arrived, grads, plan = layer_call(
        block_rows, block_cols, block_count, recv_lists, features.T, cotangent.T, degree.reshape(NB, BS),
        w_self, w_neigh, bias_terms, block_vals,
    )
    hidden, grad_features, grad_self, grad_neigh = results_call(plan, base, arrived, hidden, grads)
    return hidden.T, grad_features.T, grad_self, grad_neigh


def solution(mesh):
    placed = (
        P("vtx", "feat"), P("feat", None), P("feat", None), P("feat"), P("vtx", None, None), P("vtx"), P("vtx"), P("vtx"),
        P("vtx"), P("vtx"), P("vtx", "feat"),
    )
    return jax.shard_map(
        on_device,
        mesh=mesh,
        in_specs=placed,
        out_specs=(P("vtx", "feat"), P("vtx", "feat"), P("feat", None), P("feat", None)),
        check_vma=False,
    )
```

time: 121 us -> 101 us (0.83)
  the two profiles are of different devices: /device:TPU:1 before, /device:TPU:13 now
where the time goes in v3:
time: 101 us; the launch traced here: 100 us
  Pallas kernels  92.8 us (92%)
  local copies, waits for them, and re-layouts  6.06 us (6%)
  between operations  1.46 us (1%)
    pallas_call x1, Pallas kernels, layer_call(): pl.pallas_call(layer_kernel, out_shape=(jax.ShapeDtypeStruct((HC, ROWS),...  89.7 us
    unnamed x10, local copies, waits for them, and re-layouts  6.06 us
    pallas_call x1, Pallas kernels, results_call(): pl.pallas_call(results_kernel, out_shape=(jax.ShapeDtypeStruct((HC, ROWS)...  3.1 us

profile of v3, /device:TPU:13, one launch (start us, length us, event | category | flops | bytes accessed | tf_op | source)
XLA Modules:
  0.0 100.3 jit_solution(503138726094135924)
XLA Ops:
  1.3 89.7 %layer.1 = (bf16[64,4096]{1,0:T(8,128)(2,1)}, f32[32,192,128]{2,1,0:T(8,128)}, bf16[2,16,192,128]{3,2,1,0:T(8,128)(2,1)}, f32[8,96,128]{2,1,0:T(8,128)}, s32[16,384]{1,0:T(8,128)}) custom-call(s32[320]{0:T(512)} %rows_hbm.1, s32[320]{0:T(512)} %cols_hbm.1, s32[1]{0:T(128)S(6)} %copy.15.count_ref, s32[32]{0:T(128)} %lists_hbm.1, bf16[192,4096]{1,0:T(8,128)(2,1)} %bitcast.5, ...), custom_call_target="tpu_custom_call" | custom-call | tf_op jit(solution)/shard_map/layer/pallas_call | solution.py:443
  91.0 0.0 copy-start
  91.0 1.9 %copy-done = f32[32,192,128]{2,1,0:T(8,128)S(1)} copy-done((f32[32,192,128]{2,1,0:T(8,128)S(1)}, f32[32,192,128]{2,1,0:T(8,128)}, u32[]{:S(2)}) %copy-start) | copy-done | bytes 3145752
  92.9 0.0 copy-start.1
  92.9 1.4 %copy-done.1 = bf16[2,16,192,128]{3,2,1,0:T(8,128)(2,1)S(1)} copy-done((bf16[2,16,192,128]{3,2,1,0:T(8,128)(2,1)S(1)}, bf16[2,16,192,128]{3,2,1,0:T(8,128)(2,1)}, u32[]{:S(2)}) %copy-start.1) | copy-done | bytes 1572888
  94.3 0.0 copy-start.2
  94.3 1.0 %copy-done.2 = bf16[64,4096]{1,0:T(8,128)(2,1)S(1)} copy-done((bf16[64,4096]{1,0:T(8,128)(2,1)S(1)}, bf16[64,4096]{1,0:T(8,128)(2,1)}, u32[]{:S(2)}) %copy-start.2) | copy-done | bytes 524312
  95.3 0.0 copy-start.3
  95.3 1.0 copy-done.3
  96.3 0.0 copy-start.4
  96.3 0.7 copy-done.4
  97.1 3.1 %results.1 = (bf16[64,4096]{1,0:T(8,128)(2,1)}, bf16[192,4096]{1,0:T(8,128)(2,1)}, f32[192,256]{1,0:T(8,128)}, f32[192,256]{1,0:T(8,128)}) custom-call(s32[16,384]{1,0:T(8,128)S(1)} %copy-done.4, f32[32,192,128]{2,1,0:T(8,128)S(1)} %copy-done, bf16[2,16,192,128]{3,2,1,0:T(8,128)(2,1)S(1)} %copy-done.1, bf16[64,4096]{1,0:T(8,128)(2,1)S(1)} %copy-done.2, ...), custom_call_target="tpu_custom_call" | custom-call | tf_op jit(solution)/shard_map/results/pallas_call | solution.py:536
Async XLA Ops:
  91.0 1.9 %copy-start = (f32[32,192,128]{2,1,0:T(8,128)S(1)}, f32[32,192,128]{2,1,0:T(8,128)}, u32[]{:S(2)}) copy-start(f32[32,192,128]{2,1,0:T(8,128)} %get-tuple-element.14.base_hbm) | copy-start | bytes 9437188
  92.9 1.4 %copy-start.1 = (bf16[2,16,192,128]{3,2,1,0:T(8,128)(2,1)S(1)}, bf16[2,16,192,128]{3,2,1,0:T(8,128)(2,1)}, u32[]{:S(2)}) copy-start(bf16[2,16,192,128]{3,2,1,0:T(8,128)(2,1)} %get-tuple-element.15.arrived_hbm) | copy-start | bytes 4718596
  94.3 1.0 %copy-start.2 = (bf16[64,4096]{1,0:T(8,128)(2,1)S(1)}, bf16[64,4096]{1,0:T(8,128)(2,1)}, u32[]{:S(2)}) copy-start(bf16[64,4096]{1,0:T(8,128)(2,1)} %get-tuple-element.16.hidden_in) | copy-start | bytes 1572868
  95.3 1.0 copy-start.3
  96.3 0.7 copy-start.4

commit v4 on v3

--- a/solution.py
+++ b/solution.py
@@ -25,10 +25,10 @@
 PAIRS_F = (NNZ + NB) // 2
 PAIRS_B = (NNZ + EXT) // 2
 PIECE_PAIRS = PAIRS_F // PIECES
-GROUP = 24
+QUARTER = (NNZ + 2 * HALO) // 8
+REST = PAIRS_B - 4 * QUARTER
 ZERO = NB
 SL_A = 4 * FC // 8
-SL_B = SL_A // 4
 MB = 1 << 20
 
 
@@ -80,6 +80,23 @@
     at_place = down(jnp.where((place_col == lane) & (block < NB), block, 0))
     of_entry = down(jnp.where(block == key, place_col, 0))
     return place, at_place, of_entry
+
+
+def order_slots(key):
+    slot, lane = iota((EXT, ENT), 0), iota((EXT, ENT), 1)
+    size = group_sizes(key)
+    size_row = down(jnp.where(slot == lane, size, 0))
+    earlier = (size < size_row) | ((size == size_row) & (slot < lane))
+    side = jnp.where(slot < HALO, 0, jnp.where(slot < HALO + NB, 1, 2))
+    lane_side = jnp.where(lane < HALO, 0, jnp.where(lane < HALO + NB, 1, 2))
+    at_side = as_column(down(jnp.where(earlier & (side == lane_side), 1, 0)))[:EXT]
+    slot, side = slot[:, :1], side[:, :1]
+    turn = ((at_side >> 2) << 3) + (at_side & 3)
+    order = jnp.where(side == 1, 2 * HALO + slot - HALO, turn + jnp.where(side == 2, 4, 0))
+    of_entry = down(jnp.where(iota((EXT, ENT), 0) == key, order, 0))
+    told = iota((EXT, BS), 1)
+    told = jnp.where(told < HALO, told, told + NB)
+    return of_entry, down(jnp.where(iota((EXT, BS), 0) == told, at_side, 0))
 
 
 def pair_schedule(key, other, active):
@@ -106,35 +123,36 @@
     return [jnp.clip(entry, 0, NNZ), jnp.clip(source, 0, EXT), goes_on, jnp.clip(done, 0, PAIRS_B)]
 
 
-def inverse(lists, first):
-    ours = as_column(lists)
+def inverse(lists, places, first):
+    ours, place = as_column(lists), as_column(places)
     sub, lane = iota((BS, BS), 0), iota((BS, BS), 1)
     hit = (ours == lane) & (sub >= first) & (sub < first + HALO)
-    return jnp.clip(down(jnp.where(hit, sub - (first + HALO), 0)) + HALO, 0, HALO)
+    return jnp.clip(down(jnp.where(hit, place - HALO, 0)) + HALO, 0, HALO)
 
 
 def layer_kernel(
     rows_hbm, cols_hbm, count_ref, lists_hbm, feat_hbm, cot_hbm, degree_hbm, ws_ref, wn_ref, bias_hbm, vals_hbm,
     hidden_hbm, base_hbm, arrived, grads_hbm, plan_hbm,
-    rows_v, cols_v, lists_v, bias_v, degree_v, rdeg, lists_out, lists_in, lists_sm, plan_v, plan,
+    rows_v, cols_v, lists_v, bias_v, degree_v, rdeg, lists_out, lists_in, lists_sm, places_out, places_in, plan_v, plan,
     ext, landed_halo, cot, vals, sums, sent, mean, wst, wnt, part, staged, landed, slopes, hid, back, base, hidden,
-    total, grads, land_a, sum_a, land_b, sum_b, whole,
+    total, grads, land_a, sum_a, whole,
     small_sem, feat_sem, cot_sem, vals_sem, sm_sem, ls, lr, hs, hr,
-    send_sem, recv_sem, bs, br, as_, ar, zs, zr, cs, cr, ds, dr, out_sem,
+    send_sem, recv_sem, bs, br, as_, ar, zs, zr, ds, dr, out_sem,
 ):
     me = lax.axis_index("feat")
     right, left = lax.rem(me + 1, NF), lax.rem(me + NF - 1, NF)
     v = lax.axis_index("vtx")
     v_right, v_left = lax.rem(v + 1, NV), lax.rem(v + NV - 1, NV)
-    h, z = lax.rem(v, 8), v // 8
-
-    def h_peer(k):
-        other = lax.rem(h + k, 8)
-        return other, {"vtx": z * 8 + other}
-
-    def z_peer(k):
-        other = lax.rem(z + k, 4)
-        return other, {"vtx": other * 8 + h}
+    core, x, z = lax.rem(v, 2), lax.rem(v // 2, 4), v // 8
+    g = 2 * z + core
+
+    def g_peer(k):
+        other = lax.rem(g + k, 8)
+        return other, {"vtx": ((other // 2) * 4 + x) * 2 + lax.rem(other, 2)}
+
+    def x_peer(k):
+        other = lax.rem(x + k, 4)
+        return other, {"vtx": (z * 4 + other) * 2 + core}
 
     small = [
         pltpu.make_async_copy(src, dst, small_sem.at[k])
@@ -158,8 +176,8 @@
     barrier = pltpu.get_barrier_semaphore()
     peers = (
         [{"vtx": v_left}, {"vtx": v_right}, {"feat": left}, {"feat": right}]
-        + [h_peer(k)[1] for k in range(1, 8)]
-        + [z_peer(k)[1] for k in range(1, 4)]
+        + [g_peer(k)[1] for k in range(1, 8)]
+        + [x_peer(k)[1] for k in range(1, 4)]
     )
     for peer in peers:
         pl.semaphore_signal(barrier, inc=1, device_id=peer, device_id_type=MESH)
@@ -212,20 +230,25 @@
     rows, cols = wide(rows_v), wide(cols_v)
     active = iota((1, ENT), 1) < count_ref[0]
     where_col = jnp.where(cols < HALO, cols + NB + 1, jnp.where(cols < HALO + NB, cols - HALO, cols + 1))
+    slot_place, places = order_slots(jnp.where(active, cols, 1000))
+    places_out[...] = jnp.broadcast_to(places, (8, BS))
+    place_trips = []
+    for k, peer in ((0, v_right), (1, v_left)):
+        trip = pltpu.make_async_remote_copy(
+            src_ref=places_out, dst_ref=places_in.at[k], send_sem=ls.at[2 + k], recv_sem=lr.at[2 + k],
+            device_id={"vtx": peer}, device_id_type=MESH,
+        )
+        trip.start()
+        place_trips.append(trip)
     place, at_place, entry_place = order_groups(jnp.where(active, rows, 1000))
-    table = pair_schedule(entry_place, where_col, active) + pair_schedule(cols, entry_place, active)
-    from_right = inverse(lists_in[1, 0:1], 0)
-    from_left = inverse(lists_in[0, 0:1], HALO)
-    table.append(jnp.concatenate([from_right, from_left, jnp.zeros((1, BS), I32)], axis=1))
-    table += [jnp.clip(place, 0, NB - 1), jnp.clip(at_place, 0, NB - 1)]
+    table = pair_schedule(entry_place, where_col, active) + pair_schedule(slot_place, entry_place, active)
+    table += [jnp.zeros((1, ENT), I32), jnp.clip(place, 0, NB - 1), jnp.clip(at_place, 0, NB - 1)]
     for k, row in enumerate(table):
         plan_v[k : k + 1] = row
     for k in range(len(table), 16):
         plan_v[k : k + 1] = jnp.zeros((1, ENT), I32)
     local = pltpu.make_async_copy(plan_v, plan, sm_sem)
     local.start()
-    plan_out = pltpu.make_async_copy(plan_v, plan_hbm, out_sem.at[0])
-    plan_out.start()
     local.wait()
 
     def block_at(q):
@@ -239,6 +262,13 @@
         pre = jnp.dot(wst[...], own, preferred_element_type=F32)
         for k in range(PB):
             part[p * PB + k] = pre[:, k * BS : (k + 1) * BS]
+    for trip in place_trips:
+        trip.wait()
+    from_right = inverse(lists_in[1, 0:1], places_in[1, 0:1], 0)
+    from_left = inverse(lists_in[0, 0:1], places_in[0, 0:1], HALO)
+    plan_v[8:9] = jnp.concatenate([from_right, from_left, jnp.zeros((1, BS), I32)], axis=1)
+    plan_out = pltpu.make_async_copy(plan_v, plan_hbm, out_sem.at[0])
+    plan_out.start()
     for load in val_loads + cot_loads:
         load.wait()
     for trip in halo_trips:
@@ -366,75 +396,70 @@
     def rows_a(k):
         return pl.ds(pl.multiple_of(k * SL_A, 32), SL_A)
 
-    def rows_b(k):
-        return pl.ds(pl.multiple_of(k * SL_B, 8), SL_B)
-
-    trips = exchange(h_peer, 7, lambda k: grads.at[rows_a(k)], land_a, h, as_, ar)
-
-    def backward_product(t):
+    a_trips = exchange(g_peer, 7, lambda k: grads.at[rows_a(k)], land_a, g, as_, ar)
+
+    def backward_pair(t, acc):
         a = jnp.concatenate([vals[plan[4, 2 * t]], vals[plan[4, 2 * t + 1]]], axis=0)
         b = side_by_side([back[plan[5, 2 * t]], back[plan[5, 2 * t + 1]]])
-        return jnp.dot(b, a, preferred_element_type=F32)
-
-    def backward_step(i, acc):
-        for u in range(GROUP):
-            t = i * GROUP + u
-            acc = acc * plan[6, 2 * t].astype(F32) + backward_product(t)
-            sums[t] = acc
+        acc = acc * plan[6, 2 * t].astype(F32) + jnp.dot(b, a, preferred_element_type=F32)
+        sums[t] = acc
         return acc
 
-    lax.fori_loop(0, PAIRS_B // GROUP, backward_step, jnp.zeros((FC, BS), F32))
-    back_trips = []
-    for q in range(4):
-        for d, towards in ((0, v_left), (1, v_right)):
-            for j in range(4 * q, 4 * q + 4):
-                sent[d, j] = sums[plan[7, (HALO + NB) * d + j]].astype(BF16)
-            trip = pltpu.make_async_remote_copy(
-                src_ref=sent.at[d, pl.ds(4 * q, 4)], dst_ref=arrived.at[d, pl.ds(4 * q, 4)],
-                send_sem=bs.at[d, q], recv_sem=br.at[d, q],
-                device_id={"vtx": towards}, device_id_type=MESH,
-            )
-            trip.start()
-            back_trips.append(trip)
-    for trip in trips:
+    def back_hop(q, d):
+        return pltpu.make_async_remote_copy(
+            src_ref=sent.at[d, pl.ds(4 * q, 4)], dst_ref=arrived.at[d, pl.ds(4 * q, 4)],
+            send_sem=bs.at[d, q], recv_sem=br.at[d, q],
+            device_id={"vtx": v_right if d else v_left}, device_id_type=MESH,
+        )
+
+    def backward_quarter(q, acc):
+        for u in range(QUARTER):
+            acc = backward_pair(q * QUARTER + u, acc)
+        for d in range(2):
+            for j in range(4):
+                sent[d, 4 * q + j] = sums[plan[7, 8 * q + 4 * d + j]].astype(BF16)
+            back_hop(q, d).start()
+        return acc
+
+    acc = lax.fori_loop(0, 3, backward_quarter, jnp.zeros((FC, BS), F32))
+    for trip in a_trips:
         trip.wait()
-    land_a[h] = grads[rows_a(h)]
-    sum_a[...] = jnp.sum(land_a[...].astype(F32), axis=0)
-    trips = exchange(z_peer, 3, lambda k: sum_a.at[rows_b(k)], land_b, z, zs, zr)
+    land_a[g] = grads[rows_a(g)]
+    sum_a[x] = jnp.sum(land_a[...].astype(F32), axis=0)
+    x_trips = exchange(x_peer, 3, lambda k: sum_a.at[x], sum_a, x, zs, zr)
+    acc = backward_quarter(3, acc)
+    for u in range(REST):
+        acc = backward_pair(4 * QUARTER + u, acc)
     for b in range(NB):
         hidden[:, b * BS : (b + 1) * BS] = hid[plan[9, b]]
     outs = [plan_out, pltpu.make_async_copy(hidden, hidden_hbm, out_sem.at[1])]
     outs[1].start()
-    for trip in trips:
+    for trip in x_trips:
         trip.wait()
-    land_b[z] = sum_a[rows_b(z)]
-    sum_b[z] = jnp.sum(land_b[...], axis=0) * float(NV * ROWS) ** -0.5
-    trips = exchange(z_peer, 3, lambda k: sum_b.at[z], sum_b, z, cs, cr)
+    whole[...] = jnp.sum(sum_a[...], axis=0) * float(NV * ROWS) ** -0.5
+    d_trips = exchange(g_peer, 7, lambda k: whole, grads_hbm, g, ds, dr)
+    outs.append(pltpu.make_async_copy(whole, grads_hbm.at[g], out_sem.at[6]))
+    outs[-1].start()
     for p in range(PIECES):
         near = jnp.dot(ws_ref[...], slopes_of(p), preferred_element_type=F32)
         for k in range(PB):
             part[p * PB + k, :FC] = near[:, k * BS : (k + 1) * BS]
-    for trip in trips:
-        trip.wait()
-    whole[h] = sum_b[...].reshape(SL_A, BS)
-    trips = exchange(h_peer, 7, lambda k: whole.at[h], whole, h, ds, dr)
     for c in range(4):
         for b in range(8 * c, 8 * c + 8):
-            base[b] = part[plan[9, b], :FC] + sums[plan[7, HALO + b]]
+            base[b] = part[plan[9, b], :FC] + sums[plan[7, 2 * HALO + b]]
         outs.append(pltpu.make_async_copy(base.at[pl.ds(8 * c, 8)], base_hbm.at[pl.ds(8 * c, 8)], out_sem.at[2 + c]))
         outs[-1].start()
-    for trip in trips:
-        trip.wait()
-    outs.append(pltpu.make_async_copy(whole, grads_hbm, out_sem.at[6]))
-    outs[-1].start()
-    for trip in back_trips:
-        trip.wait()
     for s in range(3):
         for p in range(PIECES):
             reduce_hop(p, s, way[p]).wait_send()
             gather_hop(p, s, way[p]).wait_send()
     for out in outs:
         out.wait()
+    for q in range(4):
+        for d in range(2):
+            back_hop(q, d).wait()
+    for trip in d_trips:
+        trip.wait()
 
 
 def layer_call(rows, cols, count, lists, feat, cot, degree, ws, wn, bias, vals):
@@ -461,6 +486,8 @@
             V((8, BS), I32),
             V((2, 8, BS), I32),
             pltpu.SMEM((2, 8, BS), I32),
+            V((8, BS), I32),
+            V((2, 8, BS), I32),
             V((16, ENT), I32),
             pltpu.SMEM((16, ENT), I32),
             V((EXT + 1, FC, BS), BF16),
@@ -483,13 +510,11 @@
             V((2, FC, HID), F32),
             V((4 * FC, BS), BF16),
             V((8, SL_A, BS), BF16),
+            V((4, SL_A, BS), F32),
             V((SL_A, BS), F32),
-            V((4, SL_B, BS), F32),
-            V((4, SL_B, BS), F32),
-            V((8, SL_A, BS), F32),
-            dma((5,)), dma((NB,)), dma((NB,)), dma((8,)), dma, dma((2,)), dma((2,)), dma((2, 4)), dma((2, 4)),
+            dma((5,)), dma((NB,)), dma((NB,)), dma((8,)), dma, dma((4,)), dma((4,)), dma((2, 4)), dma((2, 4)),
             dma((6, PIECES)), dma((6, PIECES)), dma((2, 4)), dma((2, 4)),
-            dma((7,)), dma((7,)), dma((3,)), dma((3,)), dma((3,)), dma((3,)), dma((7,)), dma((7,)), dma((7,)),
+            dma((7,)), dma((7,)), dma((3,)), dma((3,)), dma((7,)), dma((7,)), dma((7,)),
         ],
         compiler_params=pltpu.CompilerParams(collective_id=0, has_side_effects=True, vmem_limit_bytes=60 * MB),
         name="layer",
@@ -551,7 +576,7 @@
             V((8, SL_A, BS), F32),
             pltpu.SemaphoreType.DMA((13,)),
         ],
-        compiler_params=pltpu.CompilerParams(vmem_limit_bytes=48 * MB),
+        compiler_params=pltpu.CompilerParams(vmem_limit_bytes=60 * MB),
         name="results",
     )(plan, base, arrived, hidden, grads)
 

time: 101 us -> 105 us (1.040)
  the two profiles are of different devices: /device:TPU:13 before, /device:TPU:1 now
where the time goes in v4:
time: 105 us
  Pallas kernels  103 us (98%)
  between operations  1.45 us (1%)
    pallas_call x1, Pallas kernels, layer_call(): pl.pallas_call(layer_kernel, out_shape=(jax.ShapeDtypeStruct((HC, ROWS),...  85.4 us
    pallas_call x1, Pallas kernels, results_call(): pl.pallas_call(results_kernel, out_shape=(jax.ShapeDtypeStruct((HC, ROWS)...  17.9 us

profile of v4, /device:TPU:1, one launch (start us, length us, event | category | flops | bytes accessed | tf_op | source)
XLA Modules:
  0.0 104.7 jit_solution(15781520012834195214)
XLA Ops:
  1.3 85.4 %layer.1 = (bf16[64,4096]{1,0:T(8,128)(2,1)}, f32[32,192,128]{2,1,0:T(8,128)}, bf16[2,16,192,128]{3,2,1,0:T(8,128)(2,1)}, f32[8,96,128]{2,1,0:T(8,128)}, s32[16,384]{1,0:T(8,128)}) custom-call(s32[320]{0:T(512)} %rows_hbm.1, s32[320]{0:T(512)} %cols_hbm.1, s32[1]{0:T(128)S(6)} %copy.15.count_ref, s32[32]{0:T(128)} %lists_hbm.1, bf16[192,4096]{1,0:T(8,128)(2,1)} %bitcast.5, ...), custom_call_target="tpu_custom_call" | custom-call | tf_op jit(solution)/shard_map/layer/pallas_call | solution.py:468
  86.7 17.9 %results.1 = (bf16[64,4096]{1,0:T(8,128)(2,1)}, bf16[192,4096]{1,0:T(8,128)(2,1)}, f32[192,256]{1,0:T(8,128)}, f32[192,256]{1,0:T(8,128)}) custom-call(s32[16,384]{1,0:T(8,128)} %get-tuple-element.13.plan_hbm, f32[32,192,128]{2,1,0:T(8,128)} %get-tuple-element.14.base_hbm, bf16[2,16,192,128]{3,2,1,0:T(8,128)(2,1)} %get-tuple-element.15.arrived_hbm, ...), custom_call_target="tpu_custom_call" | custom-call | tf_op jit(solution)/shard_map/results/pallas_call | solution.py:561

commit v5 on v4

--- a/solution.py
+++ b/solution.py
@@ -436,7 +436,7 @@
     outs[1].start()
     for trip in x_trips:
         trip.wait()
-    whole[...] = jnp.sum(sum_a[...], axis=0) * float(NV * ROWS) ** -0.5
+    whole[...] = (jnp.sum(sum_a[...], axis=0) * float(NV * ROWS) ** -0.5).astype(BF16)
     d_trips = exchange(g_peer, 7, lambda k: whole, grads_hbm, g, ds, dr)
     outs.append(pltpu.make_async_copy(whole, grads_hbm.at[g], out_sem.at[6]))
     outs[-1].start()
@@ -471,7 +471,7 @@
             jax.ShapeDtypeStruct((HC, ROWS), BF16),
             jax.ShapeDtypeStruct((NB, FC, BS), F32),
             jax.ShapeDtypeStruct((2, HALO, FC, BS), BF16),
-            jax.ShapeDtypeStruct((8, SL_A, BS), F32),
+            jax.ShapeDtypeStruct((8, SL_A, BS), BF16),
             jax.ShapeDtypeStruct((16, ENT), I32),
         ),
         in_specs=[anyspace(), anyspace(), smem()] + [anyspace()] * 4 + [vmem()] * 2 + [anyspace()] * 2,
@@ -511,7 +511,7 @@
             V((4 * FC, BS), BF16),
             V((8, SL_A, BS), BF16),
             V((4, SL_A, BS), F32),
-            V((SL_A, BS), F32),
+            V((SL_A, BS), BF16),
             dma((5,)), dma((NB,)), dma((NB,)), dma((8,)), dma, dma((4,)), dma((4,)), dma((2, 4)), dma((2, 4)),
             dma((6, PIECES)), dma((6, PIECES)), dma((2, 4)), dma((2, 4)),
             dma((7,)), dma((7,)), dma((3,)), dma((3,)), dma((7,)), dma((7,)), dma((7,)),
@@ -523,36 +523,46 @@
 
 def results_kernel(
     plan_hbm, base_hbm, arrived_hbm, hidden_in, grads_hbm,
-    hidden_out, features_hbm, self_ref, neigh_ref,
-    plan, base, arrived, features, grads, sems,
+    hidden_out, features_hbm, self_hbm, neigh_hbm,
+    plan, base, arrived, features, hidden, grads, weights, sems, out_sems,
 ):
-    loads = [pltpu.make_async_copy(plan_hbm, plan, sems.at[0]), pltpu.make_async_copy(grads_hbm, grads, sems.at[1])]
-    loads += [pltpu.make_async_copy(arrived_hbm.at[d], arrived.at[d, pl.ds(0, HALO)], sems.at[2 + d]) for d in range(2)]
+    grads_load = pltpu.make_async_copy(grads_hbm, grads, sems.at[0])
+    plan_load = pltpu.make_async_copy(plan_hbm, plan, sems.at[1])
+    arrivals = [
+        pltpu.make_async_copy(arrived_hbm.at[d], arrived.at[d, pl.ds(0, HALO)], sems.at[2 + d]) for d in range(2)
+    ]
+    hidden_load = pltpu.make_async_copy(hidden_in, hidden, sems.at[4])
     pieces = [
-        pltpu.make_async_copy(base_hbm.at[pl.ds(8 * c, 8)], base.at[pl.ds(8 * c, 8)], sems.at[4 + c]) for c in range(4)
+        pltpu.make_async_copy(base_hbm.at[pl.ds(4 * c, 4)], base.at[pl.ds(4 * c, 4)], sems.at[5 + c]) for c in range(8)
     ]
-    copy = pltpu.make_async_copy(hidden_in, hidden_out, sems.at[8])
-    for load in loads + pieces + [copy]:
+    for load in [plan_load, grads_load] + arrivals + pieces[:2] + [hidden_load] + pieces[2:]:
         load.start()
     for d in range(2):
         arrived[d, HALO] = jnp.zeros((FC, BS), BF16)
-    for load in loads:
+    grads_load.wait()
+    every = grads[...].reshape(4 * FC, BS).astype(F32)
+    outs = []
+    for k, ref in ((0, self_hbm), (1, neigh_hbm)):
+        for c in range(2):
+            at = (2 * k + c) * FC
+            weights[k, :, c * BS : (c + 1) * BS] = every[at : at + FC]
+        outs.append(pltpu.make_async_copy(weights.at[k], ref, out_sems.at[k]))
+        outs[-1].start()
+    for load in [plan_load] + arrivals:
         load.wait()
-    outs = []
-    for c in range(4):
+    for c in range(8):
         pieces[c].wait()
-        for b in range(8 * c, 8 * c + 8):
+        for b in range(4 * c, 4 * c + 4):
             extra = arrived[0, plan[8, b]].astype(F32) + arrived[1, plan[8, BS + b]].astype(F32)
             features[:, b * BS : (b + 1) * BS] = (base[b] + extra).astype(BF16)
-        at = pl.ds(8 * c * BS, 8 * BS)
-        outs.append(pltpu.make_async_copy(features.at[:, at], features_hbm.at[:, at], sems.at[9 + c]))
+        at = pl.ds(4 * c * BS, 4 * BS)
+        outs.append(pltpu.make_async_copy(features.at[:, at], features_hbm.at[:, at], out_sems.at[3 + c]))
         outs[-1].start()
-    every = grads[...].reshape(4 * FC, BS)
-    for k, ref in ((0, self_ref), (1, neigh_ref)):
-        for c in range(2):
-            at = (2 * k + c) * FC
-            ref[:, c * BS : (c + 1) * BS] = every[at : at + FC]
-    for out in outs + [copy]:
+        if c == 2:
+            hidden_load.wait()
+            outs.append(pltpu.make_async_copy(hidden, hidden_out, out_sems.at[2]))
+            outs[-1].start()
+    for out in outs:
         out.wait()
 
 
@@ -567,14 +577,17 @@
             jax.ShapeDtypeStruct((FC, HID), F32),
         ),
         in_specs=[anyspace()] * 5,
-        out_specs=(anyspace(), anyspace(), vmem(), vmem()),
+        out_specs=(anyspace(),) * 4,
         scratch_shapes=[
             pltpu.SMEM((16, ENT), I32),
             V((NB, FC, BS), F32),
             V((2, HALO + 1, FC, BS), BF16),
             V((FC, ROWS), BF16),
-            V((8, SL_A, BS), F32),
+            V((HC, ROWS), BF16),
+            V((8, SL_A, BS), BF16),
+            V((2, FC, HID), F32),
             pltpu.SemaphoreType.DMA((13,)),
+            pltpu.SemaphoreType.DMA((11,)),
         ],
         compiler_params=pltpu.CompilerParams(vmem_limit_bytes=60 * MB),
         name="results",

time: 105 us -> 88.7 us (0.84)
  Pallas kernels: 103 us -> 87.1 us
    pallas_call x1, Pallas kernels: 17.9 us -> 3.8 us  [results_call(): pl.pallas_call(results_kernel, out_shape=(jax.ShapeDtypeStruct((HC, ROWS)...]
    pallas_call x1, Pallas kernels: 85.4 us -> 83.3 us  [layer_call(): pl.pallas_call(layer_kernel, out_shape=(jax.ShapeDtypeStruct((HC, ROWS),...]
where the time goes in v5:
time: 88.7 us; the launch traced here: 88.6 us
  Pallas kernels  87.1 us (98%)
  between operations  1.45 us (2%)
    pallas_call x1, Pallas kernels, layer_call(): pl.pallas_call(layer_kernel, out_shape=(jax.ShapeDtypeStruct((HC, ROWS),...  83.3 us
    pallas_call x1, Pallas kernels, results_call(): pl.pallas_call(results_kernel, out_shape=(jax.ShapeDtypeStruct((HC, ROWS)...  3.8 us

profile of v5, /device:TPU:1, one launch (start us, length us, event | category | flops | bytes accessed | tf_op | source)
XLA Modules:
  0.0 88.6 jit_solution(13125259858251643137)
XLA Ops:
  1.3 83.3 %layer.1 = (bf16[64,4096]{1,0:T(8,128)(2,1)}, f32[32,192,128]{2,1,0:T(8,128)}, bf16[2,16,192,128]{3,2,1,0:T(8,128)(2,1)}, bf16[8,96,128]{2,1,0:T(8,128)(2,1)}, s32[16,384]{1,0:T(8,128)}) custom-call(s32[320]{0:T(512)} %rows_hbm.1, s32[320]{0:T(512)} %cols_hbm.1, s32[1]{0:T(128)S(6)} %copy.15.count_ref, s32[32]{0:T(128)} %lists_hbm.1, ...), custom_call_target="tpu_custom_call" | custom-call | tf_op jit(solution)/shard_map/layer/pallas_call | solution.py:468
  84.6 3.8 %results.1 = (bf16[64,4096]{1,0:T(8,128)(2,1)}, bf16[192,4096]{1,0:T(8,128)(2,1)}, f32[192,256]{1,0:T(8,128)}, f32[192,256]{1,0:T(8,128)}) custom-call(s32[16,384]{1,0:T(8,128)} %get-tuple-element.13.plan_hbm, f32[32,192,128]{2,1,0:T(8,128)} %get-tuple-element.14.base_hbm, bf16[2,16,192,128]{3,2,1,0:T(8,128)(2,1)} %get-tuple-element.15.arrived_hbm, ...), custom_call_target="tpu_custom_call" | custom-call | tf_op jit(solution)/shard_map/results/pallas_call | solution.py:571

commit v6 on v5

--- a/solution.py
+++ b/solution.py
@@ -421,24 +421,24 @@
             back_hop(q, d).start()
         return acc
 
-    acc = lax.fori_loop(0, 3, backward_quarter, jnp.zeros((FC, BS), F32))
+    acc = lax.fori_loop(0, 2, backward_quarter, jnp.zeros((FC, BS), F32))
     for trip in a_trips:
         trip.wait()
     land_a[g] = grads[rows_a(g)]
-    sum_a[x] = jnp.sum(land_a[...].astype(F32), axis=0)
+    sum_a[x] = jnp.sum(land_a[...].astype(F32), axis=0).astype(BF16)
     x_trips = exchange(x_peer, 3, lambda k: sum_a.at[x], sum_a, x, zs, zr)
-    acc = backward_quarter(3, acc)
+    acc = lax.fori_loop(2, 4, backward_quarter, acc)
     for u in range(REST):
         acc = backward_pair(4 * QUARTER + u, acc)
+    for trip in x_trips:
+        trip.wait()
+    whole[...] = (jnp.sum(sum_a[...].astype(F32), axis=0) * float(NV * ROWS) ** -0.5).astype(BF16)
+    d_trips = exchange(g_peer, 7, lambda k: whole, grads_hbm, g, ds, dr)
+    outs = [plan_out, pltpu.make_async_copy(whole, grads_hbm.at[g], out_sem.at[6])]
+    outs[-1].start()
     for b in range(NB):
         hidden[:, b * BS : (b + 1) * BS] = hid[plan[9, b]]
-    outs = [plan_out, pltpu.make_async_copy(hidden, hidden_hbm, out_sem.at[1])]
-    outs[1].start()
-    for trip in x_trips:
-        trip.wait()
-    whole[...] = (jnp.sum(sum_a[...], axis=0) * float(NV * ROWS) ** -0.5).astype(BF16)
-    d_trips = exchange(g_peer, 7, lambda k: whole, grads_hbm, g, ds, dr)
-    outs.append(pltpu.make_async_copy(whole, grads_hbm.at[g], out_sem.at[6]))
+    outs.append(pltpu.make_async_copy(hidden, hidden_hbm, out_sem.at[1]))
     outs[-1].start()
     for p in range(PIECES):
         near = jnp.dot(ws_ref[...], slopes_of(p), preferred_element_type=F32)
@@ -510,7 +510,7 @@
             V((2, FC, HID), F32),
             V((4 * FC, BS), BF16),
             V((8, SL_A, BS), BF16),
-            V((4, SL_A, BS), F32),
+            V((4, SL_A, BS), BF16),
             V((SL_A, BS), BF16),
             dma((5,)), dma((NB,)), dma((NB,)), dma((8,)), dma, dma((4,)), dma((4,)), dma((2, 4)), dma((2, 4)),
             dma((6, PIECES)), dma((6, PIECES)), dma((2, 4)), dma((2, 4)),

time: 88.7 us -> 87.8 us (0.990)
  Pallas kernels: 87.1 us -> 86.1 us
    pallas_call x1, Pallas kernels: 83.3 us -> 82.2 us  [layer_call(): pl.pallas_call(layer_kernel, out_shape=(jax.ShapeDtypeStruct((HC, ROWS),...]
where the time goes in v6:
time: 87.8 us; the launch traced here: 87.5 us
  Pallas kernels  86.1 us (98%)
  between operations  1.45 us (2%)
    pallas_call x1, Pallas kernels, layer_call(): pl.pallas_call(layer_kernel, out_shape=(jax.ShapeDtypeStruct((HC, ROWS),...  82.2 us
    pallas_call x1, Pallas kernels, results_call(): pl.pallas_call(results_kernel, out_shape=(jax.ShapeDtypeStruct((HC, ROWS)...  3.8 us

profile of v6, /device:TPU:1, one launch (start us, length us, event | category | flops | bytes accessed | tf_op | source)
XLA Modules:
  0.0 87.5 jit_solution(4913541443130365868)
XLA Ops:
  1.3 82.2 %layer.1 = (bf16[64,4096]{1,0:T(8,128)(2,1)}, f32[32,192,128]{2,1,0:T(8,128)}, bf16[2,16,192,128]{3,2,1,0:T(8,128)(2,1)}, bf16[8,96,128]{2,1,0:T(8,128)(2,1)}, s32[16,384]{1,0:T(8,128)}) custom-call(s32[320]{0:T(512)} %rows_hbm.1, s32[320]{0:T(512)} %cols_hbm.1, s32[1]{0:T(128)S(6)} %copy.15.count_ref, s32[32]{0:T(128)} %lists_hbm.1, ...), custom_call_target="tpu_custom_call" | custom-call | tf_op jit(solution)/shard_map/layer/pallas_call | solution.py:468
  83.5 3.8 %results.1 = (bf16[64,4096]{1,0:T(8,128)(2,1)}, bf16[192,4096]{1,0:T(8,128)(2,1)}, f32[192,256]{1,0:T(8,128)}, f32[192,256]{1,0:T(8,128)}) custom-call(s32[16,384]{1,0:T(8,128)} %get-tuple-element.13.plan_hbm, f32[32,192,128]{2,1,0:T(8,128)} %get-tuple-element.14.base_hbm, bf16[2,16,192,128]{3,2,1,0:T(8,128)(2,1)} %get-tuple-element.15.arrived_hbm, ...), custom_call_target="tpu_custom_call" | custom-call | tf_op jit(solution)/shard_map/results/pallas_call | solution.py:571

commit v7 on v6

--- a/solution.py
+++ b/solution.py
@@ -132,9 +132,9 @@
 
 def layer_kernel(
     rows_hbm, cols_hbm, count_ref, lists_hbm, feat_hbm, cot_hbm, degree_hbm, ws_ref, wn_ref, bias_hbm, vals_hbm,
-    hidden_hbm, base_hbm, arrived, grads_hbm, plan_hbm,
+    hidden_hbm, features_hbm, grads_hbm,
     rows_v, cols_v, lists_v, bias_v, degree_v, rdeg, lists_out, lists_in, lists_sm, places_out, places_in, plan_v, plan,
-    ext, landed_halo, cot, vals, sums, sent, mean, wst, wnt, part, staged, landed, slopes, hid, back, base, hidden,
+    ext, landed_halo, cot, vals, sums, sent, mean, wst, wnt, part, staged, landed, slopes, hid, back, base, hidden, arrived, features,
     total, grads, land_a, sum_a, whole,
     small_sem, feat_sem, cot_sem, vals_sem, sm_sem, ls, lr, hs, hr,
     send_sem, recv_sem, bs, br, as_, ar, zs, zr, ds, dr, out_sem,
@@ -267,8 +267,11 @@
     from_right = inverse(lists_in[1, 0:1], places_in[1, 0:1], 0)
     from_left = inverse(lists_in[0, 0:1], places_in[0, 0:1], HALO)
     plan_v[8:9] = jnp.concatenate([from_right, from_left, jnp.zeros((1, BS), I32)], axis=1)
-    plan_out = pltpu.make_async_copy(plan_v, plan_hbm, out_sem.at[0])
-    plan_out.start()
+    local = pltpu.make_async_copy(plan_v.at[pl.ds(8, 8)], plan.at[pl.ds(8, 8)], sm_sem)
+    local.start()
+    for d in range(2):
+        arrived[d, HALO] = jnp.zeros((FC, BS), BF16)
+    local.wait()
     for load in val_loads + cot_loads:
         load.wait()
     for trip in halo_trips:
@@ -365,13 +368,18 @@
     def slopes_of(p):
         return side_by_side([slopes[p, :, k].reshape(HID, BS) for k in range(PB)])
 
-    for p in range(PIECES):
-        gather_hop(p, 2, way[p]).wait_recv()
-        full = slopes_of(p)
+
+    def back_of(p, full):
         far = jnp.dot(wn_ref[...], full, preferred_element_type=F32)
         for k in range(PB):
             q = p * PB + k
             back[q] = (far[:, k * BS : (k + 1) * BS] * rdeg[block_at(q)][0:1]).astype(BF16)
+
+    for p in range(PIECES):
+        gather_hop(p, 2, way[p]).wait_recv()
+        full = slopes_of(p)
+        if p < PIECES - 2:
+            back_of(p, full)
         own = side_by_side([ext[block_at(p * PB + k)] for k in range(PB)])
         near = side_by_side([mean[p * PB + k] for k in range(PB)])
         total[0] += lax.dot_general(own, full, lanes, preferred_element_type=F32)
@@ -397,6 +405,8 @@
         return pl.ds(pl.multiple_of(k * SL_A, 32), SL_A)
 
     a_trips = exchange(g_peer, 7, lambda k: grads.at[rows_a(k)], land_a, g, as_, ar)
+    for p in range(PIECES - 2, PIECES):
+        back_of(p, slopes_of(p))
 
     def backward_pair(t, acc):
         a = jnp.concatenate([vals[plan[4, 2 * t]], vals[plan[4, 2 * t + 1]]], axis=0)
@@ -434,7 +444,7 @@
         trip.wait()
     whole[...] = (jnp.sum(sum_a[...].astype(F32), axis=0) * float(NV * ROWS) ** -0.5).astype(BF16)
     d_trips = exchange(g_peer, 7, lambda k: whole, grads_hbm, g, ds, dr)
-    outs = [plan_out, pltpu.make_async_copy(whole, grads_hbm.at[g], out_sem.at[6])]
+    outs = [pltpu.make_async_copy(whole, grads_hbm.at[g], out_sem.at[6])]
     outs[-1].start()
     for b in range(NB):
         hidden[:, b * BS : (b + 1) * BS] = hid[plan[9, b]]
@@ -444,20 +454,24 @@
         near = jnp.dot(ws_ref[...], slopes_of(p), preferred_element_type=F32)
         for k in range(PB):
             part[p * PB + k, :FC] = near[:, k * BS : (k + 1) * BS]
-    for c in range(4):
-        for b in range(8 * c, 8 * c + 8):
-            base[b] = part[plan[9, b], :FC] + sums[plan[7, 2 * HALO + b]]
-        outs.append(pltpu.make_async_copy(base.at[pl.ds(8 * c, 8)], base_hbm.at[pl.ds(8 * c, 8)], out_sem.at[2 + c]))
-        outs[-1].start()
+    for b in range(NB):
+        base[b] = part[plan[9, b], :FC] + sums[plan[7, 2 * HALO + b]]
     for s in range(3):
         for p in range(PIECES):
             reduce_hop(p, s, way[p]).wait_send()
             gather_hop(p, s, way[p]).wait_send()
-    for out in outs:
-        out.wait()
     for q in range(4):
         for d in range(2):
             back_hop(q, d).wait()
+    for c in range(4):
+        for b in range(8 * c, 8 * c + 8):
+            extra = arrived[0, plan[8, b]].astype(F32) + arrived[1, plan[8, BS + b]].astype(F32)
+            features[:, b * BS : (b + 1) * BS] = (base[b] + extra).astype(BF16)
+        at = pl.ds(8 * c * BS, 8 * BS)
+        outs.append(pltpu.make_async_copy(features.at[:, at], features_hbm.at[:, at], out_sem.at[2 + c]))
+        outs[-1].start()
+    for out in outs:
+        out.wait()
     for trip in d_trips:
         trip.wait()
 
@@ -469,13 +483,11 @@
         layer_kernel,
         out_shape=(
             jax.ShapeDtypeStruct((HC, ROWS), BF16),
-            jax.ShapeDtypeStruct((NB, FC, BS), F32),
-            jax.ShapeDtypeStruct((2, HALO, FC, BS), BF16),
+            jax.ShapeDtypeStruct((FC, ROWS), BF16),
             jax.ShapeDtypeStruct((8, SL_A, BS), BF16),
-            jax.ShapeDtypeStruct((16, ENT), I32),
         ),
         in_specs=[anyspace(), anyspace(), smem()] + [anyspace()] * 4 + [vmem()] * 2 + [anyspace()] * 2,
-        out_specs=(anyspace(),) * 5,
+        out_specs=(anyspace(),) * 3,
         scratch_shapes=[
             V((NNZ,), I32),
             V((NNZ,), I32),
@@ -507,6 +519,8 @@
             V((NB, FC, BS), BF16),
             V((NB, FC, BS), F32),
             V((HC, ROWS), BF16),
+            V((2, HALO + 1, FC, BS), BF16),
+            V((FC, ROWS), BF16),
             V((2, FC, HID), F32),
             V((4 * FC, BS), BF16),
             V((8, SL_A, BS), BF16),
@@ -522,51 +536,36 @@
 
 
 def results_kernel(
-    plan_hbm, base_hbm, arrived_hbm, hidden_in, grads_hbm,
-    hidden_out, features_hbm, self_hbm, neigh_hbm,
-    plan, base, arrived, features, hidden, grads, weights, sems, out_sems,
+    features_in, hidden_in, grads_hbm, hidden_out, features_out, self_hbm, neigh_hbm,
+    features, hidden, grads, weights, in_sems, out_sems,
 ):
-    grads_load = pltpu.make_async_copy(grads_hbm, grads, sems.at[0])
-    plan_load = pltpu.make_async_copy(plan_hbm, plan, sems.at[1])
-    arrivals = [
-        pltpu.make_async_copy(arrived_hbm.at[d], arrived.at[d, pl.ds(0, HALO)], sems.at[2 + d]) for d in range(2)
-    ]
-    hidden_load = pltpu.make_async_copy(hidden_in, hidden, sems.at[4])
-    pieces = [
-        pltpu.make_async_copy(base_hbm.at[pl.ds(4 * c, 4)], base.at[pl.ds(4 * c, 4)], sems.at[5 + c]) for c in range(8)
-    ]
-    for load in [plan_load, grads_load] + arrivals + pieces[:2] + [hidden_load] + pieces[2:]:
+    share = FC // 4
+    routes = [(hidden_in, hidden, hidden_out)]
+    for c in range(4):
+        at = pl.ds(c * share, share)
+        routes.append((features_in.at[at], features.at[at], features_out.at[at]))
+    grads_load = pltpu.make_async_copy(grads_hbm, grads, in_sems.at[5])
+    grads_load.start()
+    loads = [pltpu.make_async_copy(src, via, in_sems.at[k]) for k, (src, via, dst) in enumerate(routes)]
+    outs = [pltpu.make_async_copy(via, dst, out_sems.at[k]) for k, (src, via, dst) in enumerate(routes)]
+    for load in loads:
         load.start()
-    for d in range(2):
-        arrived[d, HALO] = jnp.zeros((FC, BS), BF16)
     grads_load.wait()
     every = grads[...].reshape(4 * FC, BS).astype(F32)
-    outs = []
     for k, ref in ((0, self_hbm), (1, neigh_hbm)):
         for c in range(2):
             at = (2 * k + c) * FC
             weights[k, :, c * BS : (c + 1) * BS] = every[at : at + FC]
-        outs.append(pltpu.make_async_copy(weights.at[k], ref, out_sems.at[k]))
+        outs.append(pltpu.make_async_copy(weights.at[k], ref, out_sems.at[5 + k]))
         outs[-1].start()
-    for load in [plan_load] + arrivals:
-        load.wait()
-    for c in range(8):
-        pieces[c].wait()
-        for b in range(4 * c, 4 * c + 4):
-            extra = arrived[0, plan[8, b]].astype(F32) + arrived[1, plan[8, BS + b]].astype(F32)
-            features[:, b * BS : (b + 1) * BS] = (base[b] + extra).astype(BF16)
-        at = pl.ds(4 * c * BS, 4 * BS)
-        outs.append(pltpu.make_async_copy(features.at[:, at], features_hbm.at[:, at], out_sems.at[3 + c]))
-        outs[-1].start()
-        if c == 2:
-            hidden_load.wait()
-            outs.append(pltpu.make_async_copy(hidden, hidden_out, out_sems.at[2]))
-            outs[-1].start()
+    for k in range(5):
+        loads[k].wait()
+        outs[k].start()
     for out in outs:
         out.wait()
 
 
-def results_call(plan, base, arrived, hidden, grads):
+def results_call(features, hidden, grads):
     V = pltpu.VMEM
     return pl.pallas_call(
         results_kernel,
@@ -576,32 +575,29 @@
             jax.ShapeDtypeStruct((FC, HID), F32),
             jax.ShapeDtypeStruct((FC, HID), F32),
         ),
-        in_specs=[anyspace()] * 5,
+        in_specs=[anyspace()] * 3,
         out_specs=(anyspace(),) * 4,
         scratch_shapes=[
-            pltpu.SMEM((16, ENT), I32),
-            V((NB, FC, BS), F32),
-            V((2, HALO + 1, FC, BS), BF16),
             V((FC, ROWS), BF16),
             V((HC, ROWS), BF16),
             V((8, SL_A, BS), BF16),
             V((2, FC, HID), F32),
-            pltpu.SemaphoreType.DMA((13,)),
-            pltpu.SemaphoreType.DMA((11,)),
+            pltpu.SemaphoreType.DMA((6,)),
+            pltpu.SemaphoreType.DMA((7,)),
         ],
         compiler_params=pltpu.CompilerParams(vmem_limit_bytes=60 * MB),
         name="results",
-    )(plan, base, arrived, hidden, grads)
+    )(features, hidden, grads)
 
 
 def on_device(
     features, w_self, w_neigh, bias_terms, block_vals, block_rows, block_cols, block_count, recv_lists, degree, cotangent
 ):
-    hidden, base, arrived, grads, plan = layer_call(
+    hidden, grad_features, grads = layer_call(
         block_rows, block_cols, block_count, recv_lists, features.T, cotangent.T, degree.reshape(NB, BS),
         w_self, w_neigh, bias_terms, block_vals,
     )
-    hidden, grad_features, grad_self, grad_neigh = results_call(plan, base, arrived, hidden, grads)
+    hidden, grad_features, grad_self, grad_neigh = results_call(grad_features, hidden, grads)
     return hidden.T, grad_features.T, grad_self, grad_neigh
 
 

time: 87.8 us -> 87.4 us (level)
    pallas_call x1, Pallas kernels: 3.8 us -> 2.57 us  [results_call(): pl.pallas_call(results_kernel, out_shape=(jax.ShapeDtypeStruct((HC, ROWS)...]
    pallas_call x1, Pallas kernels: 82.2 us -> 83.1 us  [layer_call(): pl.pallas_call(layer_kernel, out_shape=(jax.ShapeDtypeStruct((HC, ROWS),...]
where the time goes in v7:
time: 87.4 us; the launch traced here: 87.2 us
  Pallas kernels  85.7 us (98%)
  between operations  1.45 us (2%)
    pallas_call x1, Pallas kernels, layer_call(): pl.pallas_call(layer_kernel, out_shape=(jax.ShapeDtypeStruct((HC, ROWS),...  83.1 us
    pallas_call x1, Pallas kernels, results_call(): pl.pallas_call(results_kernel, out_shape=(jax.ShapeDtypeStruct((HC, ROWS)...  2.57 us

profile of v7, /device:TPU:1, one launch (start us, length us, event | category | flops | bytes accessed | tf_op | source)
XLA Modules:
  0.0 87.2 jit_solution(5995410160952250132)
XLA Ops:
  1.3 83.1 %layer.1 = (bf16[64,4096]{1,0:T(8,128)(2,1)}, bf16[192,4096]{1,0:T(8,128)(2,1)}, bf16[8,96,128]{2,1,0:T(8,128)(2,1)}) custom-call(s32[320]{0:T(512)} %rows_hbm.1, s32[320]{0:T(512)} %cols_hbm.1, s32[1]{0:T(128)S(6)} %copy.15.count_ref, s32[32]{0:T(128)} %lists_hbm.1, bf16[192,4096]{1,0:T(8,128)(2,1)} %bitcast.5, bf16[64,4096]{1,0:T(8,128)(2,1)} %bitcast.6, ...), custom_call_target="tpu_custom_call" | custom-call | tf_op jit(solution)/shard_map/layer/pallas_call | solution.py:482
  84.4 2.6 %results.1 = (bf16[64,4096]{1,0:T(8,128)(2,1)}, bf16[192,4096]{1,0:T(8,128)(2,1)}, f32[192,256]{1,0:T(8,128)}, f32[192,256]{1,0:T(8,128)}) custom-call(bf16[192,4096]{1,0:T(8,128)(2,1)} %get-tuple-element.11.features_in, bf16[64,4096]{1,0:T(8,128)(2,1)} %get-tuple-element.12.hidden_in, bf16[8,96,128]{2,1,0:T(8,128)(2,1)} %get-tuple-element.13.grads_hbm), custom_call_target="tpu_custom_call" | custom-call | tf_op jit(solution)/shard_map/results/pallas_call | solution.py:570

commit v8 on v7

--- a/solution.py
+++ b/solution.py
@@ -368,18 +368,13 @@
     def slopes_of(p):
         return side_by_side([slopes[p, :, k].reshape(HID, BS) for k in range(PB)])
 
-
-    def back_of(p, full):
+    for p in range(PIECES):
+        gather_hop(p, 2, way[p]).wait_recv()
+        full = slopes_of(p)
         far = jnp.dot(wn_ref[...], full, preferred_element_type=F32)
         for k in range(PB):
             q = p * PB + k
             back[q] = (far[:, k * BS : (k + 1) * BS] * rdeg[block_at(q)][0:1]).astype(BF16)
-
-    for p in range(PIECES):
-        gather_hop(p, 2, way[p]).wait_recv()
-        full = slopes_of(p)
-        if p < PIECES - 2:
-            back_of(p, full)
         own = side_by_side([ext[block_at(p * PB + k)] for k in range(PB)])
         near = side_by_side([mean[p * PB + k] for k in range(PB)])
         total[0] += lax.dot_general(own, full, lanes, preferred_element_type=F32)
@@ -405,8 +400,6 @@
         return pl.ds(pl.multiple_of(k * SL_A, 32), SL_A)
 
     a_trips = exchange(g_peer, 7, lambda k: grads.at[rows_a(k)], land_a, g, as_, ar)
-    for p in range(PIECES - 2, PIECES):
-        back_of(p, slopes_of(p))
 
     def backward_pair(t, acc):
         a = jnp.concatenate([vals[plan[4, 2 * t]], vals[plan[4, 2 * t + 1]]], axis=0)

time: 87.4 us -> 87.2 us (level)
  no operation moved by 1% of the time
where the time goes in v8:
time: 87.2 us; the launch traced here: 87 us
  Pallas kernels  85.6 us (98%)
  between operations  1.45 us (2%)
    pallas_call x1, Pallas kernels, layer_call(): pl.pallas_call(layer_kernel, out_shape=(jax.ShapeDtypeStruct((HC, ROWS),...  83 us
    pallas_call x1, Pallas kernels, results_call(): pl.pallas_call(results_kernel, out_shape=(jax.ShapeDtypeStruct((HC, ROWS)...  2.57 us

profile of v8, /device:TPU:1, one launch (start us, length us, event | category | flops | bytes accessed | tf_op | source)
XLA Modules:
  0.0 87.0 jit_solution(1266540455806202861)
XLA Ops:
  1.3 83.0 %layer.1 = (bf16[64,4096]{1,0:T(8,128)(2,1)}, bf16[192,4096]{1,0:T(8,128)(2,1)}, bf16[8,96,128]{2,1,0:T(8,128)(2,1)}) custom-call(s32[320]{0:T(512)} %rows_hbm.1, s32[320]{0:T(512)} %cols_hbm.1, s32[1]{0:T(128)S(6)} %copy.15.count_ref, s32[32]{0:T(128)} %lists_hbm.1, bf16[192,4096]{1,0:T(8,128)(2,1)} %bitcast.5, bf16[64,4096]{1,0:T(8,128)(2,1)} %bitcast.6, ...), custom_call_target="tpu_custom_call" | custom-call | tf_op jit(solution)/shard_map/layer/pallas_call | solution.py:475
  84.3 2.6 %results.1 = (bf16[64,4096]{1,0:T(8,128)(2,1)}, bf16[192,4096]{1,0:T(8,128)(2,1)}, f32[192,256]{1,0:T(8,128)}, f32[192,256]{1,0:T(8,128)}) custom-call(bf16[192,4096]{1,0:T(8,128)(2,1)} %get-tuple-element.11.features_in, bf16[64,4096]{1,0:T(8,128)(2,1)} %get-tuple-element.12.hidden_in, bf16[8,96,128]{2,1,0:T(8,128)(2,1)} %get-tuple-element.13.grads_hbm), custom_call_target="tpu_custom_call" | custom-call | tf_op jit(solution)/shard_map/results/pallas_call | solution.py:563

commit v9 on v8

--- a/solution.py
+++ b/solution.py
@@ -212,17 +212,15 @@
     local.start()
     local.wait()
     halo_trips = []
-    for q in range(4):
-        for d in range(2):
-            for j in range(4 * q, 4 * q + 4):
-                sent[d, j] = ext[lax.rem(lists_sm[1 - d, 0, j + HALO * d] + NB + 1, NB + 1)]
-            trip = pltpu.make_async_remote_copy(
-                src_ref=sent.at[d, pl.ds(4 * q, 4)], dst_ref=landed_halo.at[d, pl.ds(4 * q, 4)],
-                send_sem=hs.at[d, q], recv_sem=hr.at[d, q],
-                device_id={"vtx": v_right if d == 0 else v_left}, device_id_type=MESH,
-            )
-            trip.start()
-            halo_trips.append(trip)
+    for d in range(2):
+        for j in range(HALO):
+            sent[d, j] = ext[lax.rem(lists_sm[1 - d, 0, j + HALO * d] + NB + 1, NB + 1)]
+        trip = pltpu.make_async_remote_copy(
+            src_ref=sent.at[d], dst_ref=landed_halo.at[d], send_sem=hs.at[d], recv_sem=hr.at[d],
+            device_id={"vtx": v_right if d == 0 else v_left}, device_id_type=MESH,
+        )
+        trip.start()
+        halo_trips.append(trip)
 
     def wide(ref):
         return jnp.concatenate([ref[...].reshape(1, NNZ), jnp.zeros((1, ENT - NNZ), I32)], axis=1)
@@ -519,7 +517,7 @@
             V((8, SL_A, BS), BF16),
             V((4, SL_A, BS), BF16),
             V((SL_A, BS), BF16),
-            dma((5,)), dma((NB,)), dma((NB,)), dma((8,)), dma, dma((4,)), dma((4,)), dma((2, 4)), dma((2, 4)),
+            dma((5,)), dma((NB,)), dma((NB,)), dma((8,)), dma, dma((4,)), dma((4,)), dma((2,)), dma((2,)),
             dma((6, PIECES)), dma((6, PIECES)), dma((2, 4)), dma((2, 4)),
             dma((7,)), dma((7,)), dma((3,)), dma((3,)), dma((7,)), dma((7,)), dma((7,)),
         ],

time: 87.2 us -> 87.4 us (level)
  no operation moved by 1% of the time
where the time goes in v9:
time: 87.4 us; the launch traced here: 87.2 us
  Pallas kernels  85.8 us (98%)
  between operations  1.45 us (2%)
    pallas_call x1, Pallas kernels, layer_call(): pl.pallas_call(layer_kernel, out_shape=(jax.ShapeDtypeStruct((HC, ROWS),...  83.2 us
    pallas_call x1, Pallas kernels, results_call(): pl.pallas_call(results_kernel, out_shape=(jax.ShapeDtypeStruct((HC, ROWS)...  2.57 us

profile of v9, /device:TPU:1, one launch (start us, length us, event | category | flops | bytes accessed | tf_op | source)
XLA Modules:
  0.0 87.2 jit_solution(9634293673549826147)
XLA Ops:
  1.3 83.2 %layer.1 = (bf16[64,4096]{1,0:T(8,128)(2,1)}, bf16[192,4096]{1,0:T(8,128)(2,1)}, bf16[8,96,128]{2,1,0:T(8,128)(2,1)}) custom-call(s32[320]{0:T(512)} %rows_hbm.1, s32[320]{0:T(512)} %cols_hbm.1, s32[1]{0:T(128)S(6)} %copy.15.count_ref, s32[32]{0:T(128)} %lists_hbm.1, bf16[192,4096]{1,0:T(8,128)(2,1)} %bitcast.5, bf16[64,4096]{1,0:T(8,128)(2,1)} %bitcast.6, ...), custom_call_target="tpu_custom_call" | custom-call | tf_op jit(solution)/shard_map/layer/pallas_call | solution.py:473
  84.5 2.6 %results.1 = (bf16[64,4096]{1,0:T(8,128)(2,1)}, bf16[192,4096]{1,0:T(8,128)(2,1)}, f32[192,256]{1,0:T(8,128)}, f32[192,256]{1,0:T(8,128)}) custom-call(bf16[192,4096]{1,0:T(8,128)(2,1)} %get-tuple-element.11.features_in, bf16[64,4096]{1,0:T(8,128)(2,1)} %get-tuple-element.12.hidden_in, bf16[8,96,128]{2,1,0:T(8,128)(2,1)} %get-tuple-element.13.grads_hbm), custom_call_target="tpu_custom_call" | custom-call | tf_op jit(solution)/shard_map/results/pallas_call | solution.py:561
